TPU v7x, 32 devices: a whole 2x2x4 slice. The times are simulated.
32 devices in a mesh: sweep: 2 (over y), xsec: 16 (over z, x, core).
Axes of the slice: x: 2, y: 2, z: 4, core: 2. Of those that a mesh axis runs over, the one named last changes fastest.
Arguments:
- cond_block: bfloat16 [2, 16, 2, 24, 40, 128], P('sweep', 'xsec'), may hold values from -0.15625 to 0.15625
- interior_src: bfloat16 [2, 16, 2, 4, 40, 128], P('sweep', 'xsec'), may hold values from -6 to 6
- face_index: int32 [2, 16, 16, 192], P('sweep', 'xsec'), may hold values from 0 to 255
- owner_count: int32 [2, 16, 16], P('sweep', 'xsec'), may hold values from 1 to 8, as said below
- coupling: float32 [4, 2, 2048], P('sweep', None, 'xsec'), may hold values from -1 to 1
- schur_inv: bfloat16 [4, 2, 2048, 2048], P('sweep', None, None, 'xsec'), may hold values from -0.09375 to 0.09375
Outputs:
- sweep_sol: float32 [4, 8, 2048], P('sweep', None, 'xsec')
Inputs may be any that keep to these rules, and one draw needn't show every extreme that they name: `owner_count`: every count is at least 1 and at most 8; in each sweep row some owner receives 8 live slots from every sender.
All inputs are finite; a program needn't handle non-finite values.
Results may differ from a plain program's by a relative error of at most 0.006.
Values may be sent and summed in bfloat16 or wider, within the bound.
No kernel may reach another device: no remote copies, remote signals or barrier semaphores. Data moves between devices by JAX's collectives and lax.ppermute only.
A program may use at most 64 MiB of HBM per device.

v0:
```python
from functools import partial

import jax
import jax.numpy as jnp
from jax import lax
from jax.sharding import PartitionSpec as P

CAP = 8


def from_behind(value, axis, steps):
    count = lax.axis_size(axis)
    initial, last = (max(0, -steps), min(count, count - steps))
    return lax.ppermute(value, axis, [(source, source + steps) for source in range(initial, last)])


def combine_rows(totals, pieces, first_row, schur_layer):
    return (
        jnp.dot(pieces, schur_layer[0], preferred_element_type=jnp.float32),
        jnp.dot(pieces, schur_layer[1], preferred_element_type=jnp.float32),
    )


def layer_input(loads, incoming, coupling_layer):
    real_part = loads[0] - (coupling_layer[0] * incoming[0] - coupling_layer[1] * incoming[1])
    imag_part = loads[1] - (coupling_layer[0] * incoming[1] + coupling_layer[1] * incoming[0])
    return jnp.concatenate([real_part, imag_part], 0).astype(jnp.bfloat16)


def layer_output(totals, count):
    first, second = totals
    return jnp.stack([first[:count] - second[count:], second[:count] + first[count:]], 0)


def shards(cond_block, interior_src, face_index, owner_count, coupling, schur_inv):
    layers_here = schur_inv.shape[0]
    width = schur_inv.shape[3]
    sources = interior_src.shape[3]
    n_faces = cond_block.shape[3]
    n_inner = cond_block.shape[4]
    peers = lax.axis_size("xsec")
    face_rows_len = n_faces * CAP
    couple_blocks = cond_block[0, 0].reshape(2, n_faces, n_inner, peers, CAP)
    interior = interior_src[0, 0].reshape(2, sources, n_inner, peers, CAP)

    def contract(first, second):
        return jnp.einsum("kidp,sidp->dskp", first, second, preferred_element_type=jnp.float32)

    real_part = contract(couple_blocks[0], interior[0]) - contract(couple_blocks[1], interior[1])
    imag_part = contract(couple_blocks[0], interior[1]) + contract(couple_blocks[1], interior[0])
    outgoing_rows = jnp.stack([real_part, imag_part], 1).reshape(peers, 2 * sources, face_rows_len)
    index_rows = face_index[0, 0]
    positions = jnp.arange(face_rows_len) % CAP
    live_mask = positions[None, :] < owner_count[0, 0][:, None]
    slot_ids = jnp.arange(layers_here * width)
    received = lax.all_to_all(outgoing_rows, "xsec", split_axis=0, concat_axis=0, tiled=True)
    row_count = received.shape[1]

    def add_group(group_at, running):
        values_block = lax.dynamic_slice_in_dim(received, group_at * 8, 8, 0)
        index_block = lax.dynamic_slice_in_dim(index_rows, group_at * 8, 8, 0)
        mask_block = lax.dynamic_slice_in_dim(live_mask, group_at * 8, 8, 0)
        onehot = jnp.where(
            (index_block[:, :, None] == slot_ids[None, None, :]) & mask_block[:, :, None], 1.0, 0.0
        ).astype(jnp.float32)
        return running + jnp.einsum(
            "cmf,cfz->mz", values_block, onehot, precision=lax.Precision.HIGHEST
        )

    start_sum = jnp.zeros((row_count, layers_here * width), jnp.float32)
    assembled = lax.fori_loop(0, peers // 8, add_group, start_sum)
    loads_all = assembled.reshape(2, sources, layers_here, width)
    chain = lax.axis_size("sweep")
    outgoing = jnp.zeros((2, sources, width), jnp.float32)
    layers_out = []
    for round_at in range(chain):
        incoming = from_behind(outgoing, "sweep", 1)
        carried = incoming
        layers_out = []
        for layer_at in range(layers_here):
            folder = partial(combine_rows, schur_layer=schur_inv[layer_at])
            empty = jnp.zeros((2 * sources, width), jnp.float32)
            totals = folder(
                (empty, empty),
                lax.all_gather(
                    layer_input(loads_all[:, :, layer_at], carried, coupling[layer_at]),
                    "xsec",
                    axis=1,
                    tiled=True,
                ),
                jnp.int32(0),
            )
            carried = layer_output(totals, sources)
            layers_out.append(carried)
        outgoing = carried
    solved = jnp.stack(layers_out, 0)
    return solved.reshape(layers_here, 2 * sources, width)


def solution(mesh):
    placed = (
        P("sweep", "xsec", None, None, None, None),
        P("sweep", "xsec", None, None, None, None),
        P("sweep", "xsec", None, None),
        P("sweep", "xsec", None),
        P("sweep", None, "xsec"),
        P("sweep", None, None, "xsec"),
    )
    return jax.shard_map(
        shards, mesh=mesh, in_specs=placed, out_specs=P("sweep", None, "xsec"), check_vma=False
    )
```

profile of v0, /device:TPU:4, one launch (start us, length us, event | category | flops | bytes accessed | tf_op | source)
XLA Modules:
  0.0 104.9 jit_solution(9901536361156662048)
XLA Ops:
  0.0 1.1 %fusion.48 = (bf16[1,1,1,24,40,128]{5,4,3,2,1,0:T(8,128)(2,1)S(1)}, bf16[1,1,1,24,40,128]{5,4,3,2,1,0:T(8,128)(2,1)S(1)}) fusion(bf16[1,1,2,24,40,128]{5,4,3,2,1,0:T(8,128)(2,1)} %param.8), kind=kLoop, calls=%fused_computation.82 | loop fusion | bytes 983040 | tf_op jit(solution)/shard_map/slice | solution.py:49
  1.1 0.4 copy.22
  1.5 0.8 fusion.49
  2.5 0.4 copy.24
  3.1 0.5 fusion.51
  3.6 0.5 fusion.52
  4.1 0.5 fusion.21
  4.6 0.5 fusion.20
  5.3 0.5 copy.25
  5.8 1.0 copy.26
  6.8 5.9 %all-to-all-start = ((f32[16,8,192]{2,1,0:T(8,128)}), f32[16,8,192]{2,1,0:T(8,128)S(1)}, u32[]{:S(2)}, u32[]{:S(2)}) async-start(f32[16,8,192]{2,1,0:T(8,128)} %copy.26), calls=%async_computation | async-start | bytes 262144 | tf_op jit(solution)/shard_map/all_to_all | solution.py:56
  12.7 1.3 %collective-permute-start = (f32[2,4,128]{2,1,0:T(4,128)S(1)}, f32[2,4,128]{2,1,0:T(4,128)S(1)}, u32[]{:S(2)}, u32[]{:S(2)}) collective-permute-start(f32[2,4,128]{2,1,0:T(4,128)S(1)} %broadcast_in_dim.33), channel_id=1, source_target_pairs={{0,16},{1,17},{2,18},{3,19},{4,20},{5,21},{6,22},{7,23},{8,24},{9,... | collective-permute-start | bytes 12296 | tf_op jit(solution)/shard_map/ppermute | solution.py:14
  14.1 6.5 %all-to-all-done = f32[16,8,192]{2,1,0:T(8,128)S(1)} async-done(((f32[16,8,192]{2,1,0:T(8,128)}), f32[16,8,192]{2,1,0:T(8,128)S(1)}, u32[]{:S(2)}, u32[]{:S(2)}) %all-to-all-start) | async-done | bytes 98336 | tf_op jit(solution)/shard_map/all_to_all | solution.py:56
  20.6 3.7 %while.14 = (s32[]{:T(128)}, f32[8,256]{1,0:T(8,128)S(1)}, f32[16,8,192]{2,1,0:T(8,128)S(1)}, s32[16,192]{1,0:T(8,128)S(1)}, pred[16,192]{1,0:T(8,128)(4,1)S(1)}...) while((s32[]{:T(128)}, f32[8,256]{1,0:T(8,128)S(1)}, f32[16,8,192]{2,1,0:T(8,128)S(1)}, ...), condition=%wide.region_1.2_spmd.clone, body=%wide.region_0.1_spmd.clone.sunk | while | flops 38932488 | bytes 107681 | solution.py:71
  20.6 1.8 %fusion.74 = f32[8,256]{1,0:T(8,128)S(1)} fusion(s32[8,192]{1,0:T(8,128)S(1)} %constant_dynamic-slice_fusion.4, pred[8,192]{1,0:T(8,128)(4,1)S(1)} %constant_dynamic-slice_fusion.5, f32[16,8,192]{2,1,0:T(8,128)S(1)} %get-tuple-element.227, s32[]{:T(128)S(6)} %select_n.41, f32[8,256]{1,0:T(8,128)S(1)} %get-tuple-element.217, pred[]{:T(512)S(6)} %compare.4), kind=kOutput, calls=%fused_computation.6.clone.1 | convolution fusion | flops 38932480 | bytes 92165 | tf_op jit(solution)/shard_map/while/body/eval_jaxpr/cmf,cfz->mz/dot_general | solution.py:66
  22.5 1.8 %fusion.74 = f32[8,256]{1,0:T(8,128)S(1)} fusion(s32[8,192]{1,0:T(8,128)S(1)} %constant_dynamic-slice_fusion.4, pred[8,192]{1,0:T(8,128)(4,1)S(1)} %constant_dynamic-slice_fusion.5, f32[16,8,192]{2,1,0:T(8,128)S(1)} %get-tuple-element.227, s32[]{:T(128)S(6)} %select_n.41, f32[8,256]{1,0:T(8,128)S(1)} %get-tuple-element.217, pred[]{:T(512)S(6)} %compare.4), kind=kOutput, calls=%fused_computation.6.clone.1 | convolution fusion | flops 38932480 | bytes 92165 | tf_op jit(solution)/shard_map/while/body/eval_jaxpr/cmf,cfz->mz/dot_general | solution.py:66
  24.5 18.1 %all_gather.12 = bf16[8,2048]{1,0:T(8,128)(2,1)S(1)} all-gather(bf16[8,128]{1,0:T(8,128)(2,1)S(1)} %pad_maximum_fusion.5), channel_id=1, replica_groups=mesh['sweep'=2,'xsec'=16] {'xsec'}, dimensions={1}, use_global_device_ids=true | all-gather | bytes 34816 | tf_op jit(solution)/shard_map/all_gather | solution.py:85
  42.8 0.2 fusion.36
  43.0 18.2 %all_gather.13 = bf16[8,2048]{1,0:T(8,128)(2,1)S(1)} all-gather(bf16[8,128]{1,0:T(8,128)(2,1)S(1)} %pad_maximum_fusion.6), channel_id=1, replica_groups=mesh['sweep'=2,'xsec'=16] {'xsec'}, dimensions={1}, use_global_device_ids=true | all-gather | bytes 34816 | tf_op jit(solution)/shard_map/all_gather | solution.py:85
  61.6 1.3 %collective-permute-start.1 = (f32[2,4,128]{2,1,0:T(4,128)S(1)}, f32[2,4,128]{2,1,0:T(4,128)S(1)}, u32[]{:S(2)}, u32[]{:S(2)}) collective-permute-start(f32[2,4,128]{2,1,0:T(4,128)S(1)} %pad_maximum_fusion.2), channel_id=1, source_target_pairs={{0,16},{1,17},{2,18},{3,19},{4,20},{5,21},{6,22},{7,23},{8,24},{9,... | collective-permute-start | bytes 12296 | tf_op jit(solution)/shard_map/ppermute | solution.py:14
  62.9 4.2 %collective-permute-done.1 = f32[2,4,128]{2,1,0:T(4,128)S(1)} collective-permute-done((f32[2,4,128]{2,1,0:T(4,128)S(1)}, f32[2,4,128]{2,1,0:T(4,128)S(1)}, u32[]{:S(2)}, u32[]{:S(2)}) %collective-permute-start.1) | collective-permute-done | bytes 4128 | tf_op jit(solution)/shard_map/ppermute | solution.py:14
  67.1 18.1 %all_gather.14 = bf16[8,2048]{1,0:T(8,128)(2,1)S(1)} all-gather(bf16[8,128]{1,0:T(8,128)(2,1)S(1)} %pad_maximum_fusion.7), channel_id=1, replica_groups=mesh['sweep'=2,'xsec'=16] {'xsec'}, dimensions={1}, use_global_device_ids=true | all-gather | bytes 34816 | tf_op jit(solution)/shard_map/all_gather | solution.py:85
  85.7 18.2 %all_gather.15 = bf16[8,2048]{1,0:T(8,128)(2,1)S(1)} all-gather(bf16[8,128]{1,0:T(8,128)(2,1)S(1)} %pad_maximum_fusion.8), channel_id=1, replica_groups=mesh['sweep'=2,'xsec'=16] {'xsec'}, dimensions={1}, use_global_device_ids=true | all-gather | bytes 34816 | tf_op jit(solution)/shard_map/all_gather | solution.py:85
  104.3 0.6 pad_maximum_fusion.1
  (43 shorter events, 2.0 us)
Async XLA Ops:
  5.1 8.9 %copy-start.3 = (s32[1,1,16]{2,1,0:T(1,128)S(1)}, s32[1,1,16]{2,1,0:T(1,128)}, u32[]{:S(2)}) copy-start(s32[1,1,16]{2,1,0:T(1,128)} %param.11) | copy-start | bytes 196
  5.1 9.0 %copy-start.2 = (f32[2,2,128]{2,1,0:T(2,128)S(1)}, f32[2,2,128]{2,1,0:T(2,128)}, u32[]{:S(2)}) copy-start(f32[2,2,128]{2,1,0:T(2,128)} %param.12) | copy-start | bytes 6148
  5.1 15.5 %copy-start.1 = (s32[1,1,16,192]{3,2,1,0:T(8,128)S(1)}, s32[1,1,16,192]{3,2,1,0:T(8,128)}, u32[]{:S(2)}) copy-start(s32[1,1,16,192]{3,2,1,0:T(8,128)} %param.10) | copy-start | bytes 36868
  5.8 36.8 %copy-start = (bf16[2,2,2048,128]{3,2,1,0:T(8,128)(2,1)S(1)}, bf16[2,2,2048,128]{3,2,1,0:T(8,128)(2,1)}, u32[]{:S(2)}) copy-start(bf16[2,2,2048,128]{3,2,1,0:T(8,128)(2,1)} %param.13) | copy-start | bytes 6291460
  6.8 13.9 %all-to-all-start = ((f32[16,8,192]{2,1,0:T(8,128)}), f32[16,8,192]{2,1,0:T(8,128)S(1)}, u32[]{:S(2)}, u32[]{:S(2)}) async-start(f32[16,8,192]{2,1,0:T(8,128)} %copy.26), calls=%async_computation | async-start | bytes 262144 | tf_op jit(solution)/shard_map/all_to_all | solution.py:56
  12.7 11.7 %collective-permute-start = (f32[2,4,128]{2,1,0:T(4,128)S(1)}, f32[2,4,128]{2,1,0:T(4,128)S(1)}, u32[]{:S(2)}, u32[]{:S(2)}) collective-permute-start(f32[2,4,128]{2,1,0:T(4,128)S(1)} %broadcast_in_dim.33), channel_id=1, source_target_pairs={{0,16},{1,17},{2,18},{3,19},{4,20},{5,21},{6,22},{7,23},{8,24},{9,... | collective-permute-start | bytes 12296 | tf_op jit(solution)/shard_map/ppermute | solution.py:14
  61.6 5.5 %collective-permute-start.1 = (f32[2,4,128]{2,1,0:T(4,128)S(1)}, f32[2,4,128]{2,1,0:T(4,128)S(1)}, u32[]{:S(2)}, u32[]{:S(2)}) collective-permute-start(f32[2,4,128]{2,1,0:T(4,128)S(1)} %pad_maximum_fusion.2), channel_id=1, source_target_pairs={{0,16},{1,17},{2,18},{3,19},{4,20},{5,21},{6,22},{7,23},{8,24},{9,... | collective-permute-start | bytes 12296 | tf_op jit(solution)/shard_map/ppermute | solution.py:14
where the time goes:
time: 106 us; the launch traced here: 105 us
  blocking collectives  72.7 us (69%)
  waiting for transfers between devices  10.7 us (10%)
  starting transfers between devices  8.49 us (8%)
  matrix products  7.22 us (7%)
  local copies, waits for them, and re-layouts  4.55 us (4%)
    all_gather x4, blocking collectives, shards(): lax.all_gather(layer_input(loads_all[:, :, layer_at], carried, coupling[l...  72.7 us
    all_to_all x1, waiting for transfers between devices, shards(): lax.all_to_all(outgoing_rows, 'xsec', split_axis=0, concat_axis=0, tiled=...  6.51 us
    all_to_all x1, starting transfers between devices, shards(): lax.all_to_all(outgoing_rows, 'xsec', split_axis=0, concat_axis=0, tiled=...  5.91 us
    ppermute x2, waiting for transfers between devices, from_behind(): lax.ppermute(value, axis, [(source, source + steps) for source in range(i...  4.2 us
    dot_general x2, matrix products, add_group(): jnp.einsum('cmf,cfz->mz', values_block, onehot, precision=lax.Precision.H...  3.69 us
    ppermute x2, starting transfers between devices, from_behind(): lax.ppermute(value, axis, [(source, source + steps) for source in range(i...  2.58 us
  transfers between devices with their start and end apart: 3, of which 2 were waited for; matrix products, arithmetic and copies ran while one was open for 4% of the time, Pallas kernels for 0%

commit v1 on v0

v1 whole, which is shorter than its diff:
```python
import jax
import jax.numpy as jnp
from jax import lax
from jax.sharding import PartitionSpec as P

CAP = 8


def spread(block, axes, count):
    copies = jnp.broadcast_to(block[None], (count,) + block.shape)
    return lax.all_to_all(copies, axes, split_axis=0, concat_axis=0, tiled=True)


def widen(gathered):
    return jnp.moveaxis(gathered, 0, 1).reshape(gathered.shape[1], -1)


def couple(loads, coupling_layer, carried):
    real_part = loads[0] - (coupling_layer[0] * carried[0] - coupling_layer[1] * carried[1])
    imag_part = loads[1] - (coupling_layer[0] * carried[1] + coupling_layer[1] * carried[0])
    return jnp.concatenate([real_part, imag_part], 0).astype(jnp.bfloat16)


def apply_schur(rhs, schur_layer):
    count = rhs.shape[0] // 2
    first = jnp.dot(rhs, schur_layer[0], preferred_element_type=jnp.float32)
    second = jnp.dot(rhs, schur_layer[1], preferred_element_type=jnp.float32)
    return jnp.stack([first[:count] - second[count:], second[:count] + first[count:]], 0)


def shards(cond_block, interior_src, face_index, owner_count, coupling, schur_inv):
    layers_here = schur_inv.shape[0]
    width = schur_inv.shape[3]
    sources = interior_src.shape[3]
    n_faces = cond_block.shape[3]
    n_inner = cond_block.shape[4]
    peers = lax.axis_size("xsec")
    chain = lax.axis_size("sweep")
    face_rows_len = n_faces * CAP
    couple_blocks = cond_block[0, 0].reshape(2, n_faces, n_inner, peers, CAP)
    interior = interior_src[0, 0].reshape(2, sources, n_inner, peers, CAP)

    def contract(first, second):
        return jnp.einsum("kidp,sidp->dskp", first, second, preferred_element_type=jnp.float32)

    real_part = contract(couple_blocks[0], interior[0]) - contract(couple_blocks[1], interior[1])
    imag_part = contract(couple_blocks[0], interior[1]) + contract(couple_blocks[1], interior[0])
    outgoing_rows = jnp.stack([real_part, imag_part], 1).reshape(peers, 2 * sources, face_rows_len)
    outgoing_rows = outgoing_rows.astype(jnp.bfloat16)
    index_rows = face_index[0, 0]
    positions = jnp.arange(face_rows_len) % CAP
    live_mask = positions[None, :] < owner_count[0, 0][:, None]
    slot_ids = jnp.arange(layers_here * width)
    received = lax.all_to_all(outgoing_rows, "xsec", split_axis=0, concat_axis=0, tiled=True)

    onehot = jnp.where(
        (index_rows[:, :, None] == slot_ids[None, None, :]) & live_mask[:, :, None], 1.0, 0.0
    ).astype(jnp.bfloat16)
    assembled = jnp.einsum("cmf,cfz->mz", received, onehot, preferred_element_type=jnp.float32)
    loads_all = assembled.reshape(2, sources, layers_here, width)

    coupling_high = coupling[0].astype(jnp.bfloat16)
    coupling_low = (coupling[0] - coupling_high.astype(jnp.float32)).astype(jnp.bfloat16)
    first_loads = loads_all[:, :, 0].reshape(2 * sources, width).astype(jnp.bfloat16)
    rows = jnp.concatenate([first_loads, coupling_high, coupling_low], 0)
    pad = -rows.shape[0] % 16
    rows = jnp.concatenate([rows, jnp.zeros((pad, width), jnp.bfloat16)], 0)
    whole = widen(spread(rows, "xsec", peers))
    full_loads = whole[: 2 * sources].astype(jnp.float32).reshape(2, sources, -1)
    full_coupling = (
        whole[2 * sources : 2 * sources + 2].astype(jnp.float32)
        + whole[2 * sources + 2 : 2 * sources + 4].astype(jnp.float32)
    )
    row_at = lax.axis_index("sweep")
    before = jnp.zeros((2, sources, peers * width), jnp.float32)
    for round_at in range(chain):
        if round_at:
            everyone = spread(carried.reshape(2 * sources, width).astype(jnp.bfloat16), ("sweep", "xsec"), chain * peers)
            start = jnp.maximum(row_at - 1, 0) * peers
            previous = widen(lax.dynamic_slice_in_dim(everyone, start, peers, 0)).astype(jnp.float32)
            previous = jnp.where(row_at > 0, previous, 0.0)
            before = previous.reshape(2, sources, peers * width)
        carried = apply_schur(couple(full_loads, full_coupling, before), schur_inv[0])
        layers_out = [carried]
        for layer_at in range(1, layers_here):
            rhs = couple(loads_all[:, :, layer_at], coupling[layer_at], carried)
            carried = apply_schur(widen(spread(rhs, "xsec", peers)), schur_inv[layer_at])
            layers_out.append(carried)
    solved = jnp.stack(layers_out, 0)
    return solved.reshape(layers_here, 2 * sources, width)


def solution(mesh):
    placed = (
        P("sweep", "xsec", None, None, None, None),
        P("sweep", "xsec", None, None, None, None),
        P("sweep", "xsec", None, None),
        P("sweep", "xsec", None),
        P("sweep", None, "xsec"),
        P("sweep", None, None, "xsec"),
    )
    return jax.shard_map(
        shards, mesh=mesh, in_specs=placed, out_specs=P("sweep", None, "xsec"), check_vma=False
    )
```

time: 106 us -> 66.9 us (0.63)
  the two profiles are of different devices: /device:TPU:4 before, /device:TPU:0 now
where the time goes in v1:
time: 66.9 us; the launch traced here: 66.4 us
  waiting for transfers between devices  27.5 us (41%)
  starting transfers between devices  16.8 us (25%)
  blocking collectives  9.2 us (14%)
  local copies, waits for them, and re-layouts  6.33 us (9%)
  matrix products  5.1 us (8%)
  other arithmetic  1.17 us (2%)
    all_to_all x3, waiting for transfers between devices, spread(): return lax.all_to_all(copies, axes, split_axis=0, concat_axis=0, tiled=True)  20.8 us
    all_to_all x3, starting transfers between devices, spread(): return lax.all_to_all(copies, axes, split_axis=0, concat_axis=0, tiled=True)  9.49 us
    all_to_all x1, blocking collectives, spread(): return lax.all_to_all(copies, axes, split_axis=0, concat_axis=0, tiled=True)  9.2 us
    all_to_all x1, starting transfers between devices, shards(): lax.all_to_all(outgoing_rows, 'xsec', split_axis=0, concat_axis=0, tiled=...  7.36 us
    all_to_all x1, waiting for transfers between devices, shards(): lax.all_to_all(outgoing_rows, 'xsec', split_axis=0, concat_axis=0, tiled=...  6.69 us
    dot_general x4, matrix products, contract(): jnp.einsum('kidp,sidp->dskp', first, second, preferred_element_type=jnp.f...  2.08 us
    broadcast_in_dim x4, local copies, waits for them, and re-layouts, spread(): copies = jnp.broadcast_to(block[None], (count,) + block.shape)  1.91 us
    dot_general x1, matrix products, shards(): jnp.einsum('cmf,cfz->mz', received, onehot, preferred_element_type=jnp.fl...  1.57 us
  transfers between devices with their start and end apart: 4, of which 4 were waited for; matrix products, arithmetic and copies ran while one was open for 0% of the time, Pallas kernels for 0%

profile of v1, /device:TPU:0, one launch (start us, length us, event | category | flops | bytes accessed | tf_op | source)
XLA Modules:
  0.0 66.4 jit_solution(525913877231192272)
XLA Ops:
  0.0 1.1 %fusion.46 = (bf16[1,1,1,24,40,128]{5,4,3,2,1,0:T(8,128)(2,1)S(1)}, bf16[1,1,1,24,40,128]{5,4,3,2,1,0:T(8,128)(2,1)S(1)}) fusion(bf16[1,1,2,24,40,128]{5,4,3,2,1,0:T(8,128)(2,1)} %param.6), kind=kLoop, calls=%fused_computation.92 | loop fusion | bytes 983040 | tf_op jit(solution)/shard_map/slice | solution.py:46
  1.1 0.4 copy.23
  1.5 0.8 %fusion.47 = (bf16[1,1,1,4,40,128]{5,4,3,2,1,0:T(8,128)(2,1)S(1)}, bf16[1,1,1,4,40,128]{5,4,3,2,1,0:T(8,128)(2,1)S(1)}) fusion(bf16[1,1,2,4,40,128]{5,4,3,2,1,0:T(8,128)(2,1)} %param.7), kind=kLoop, calls=%fused_computation.93 | loop fusion | bytes 163840 | tf_op jit(solution)/shard_map/slice | solution.py:46
  2.5 0.4 copy.25
  3.1 0.5 fusion.50
  3.6 0.5 fusion.51
  4.1 0.5 fusion.6
  4.6 0.5 fusion.5
  5.4 0.4 copy.26
  5.8 0.8 %copy.27 = bf16[16,8,192]{2,1,0:T(8,128)(2,1)} copy(bf16[16,8,192]{0,2,1:T(8,128)(2,1)S(1)} %bitcast.126) | data formatting | bytes 98304 | tf_op jit(solution)/shard_map/convert_element_type | solution.py:49
  6.6 7.4 %all-to-all-start = ((bf16[16,8,192]{2,1,0:T(8,128)(2,1)}), bf16[16,8,192]{2,1,0:T(8,128)(2,1)S(1)}, u32[]{:S(2)}, u32[]{:S(2)}) async-start(bf16[16,8,192]{2,1,0:T(8,128)(2,1)} %copy.27), calls=%async_computation | async-start | bytes 131072 | tf_op jit(solution)/shard_map/all_to_all | solution.py:54
  14.2 6.7 %all-to-all-done = bf16[16,8,192]{2,1,0:T(8,128)(2,1)S(1)} async-done(((bf16[16,8,192]{2,1,0:T(8,128)(2,1)}), bf16[16,8,192]{2,1,0:T(8,128)(2,1)S(1)}, u32[]{:S(2)}, u32[]{:S(2)}) %all-to-all-start) | async-done | bytes 49184 | tf_op jit(solution)/shard_map/all_to_all | solution.py:54
  20.9 1.6 %fusion.1 = f32[8,256,1]{1,0,2:T(8,128)S(1)} fusion(bf16[16,8,192]{2,1,0:T(8,128)(2,1)S(1)} %all-to-all-done, s32[16,192]{1,0:T(8,128)S(1)} %bitcast.148, pred[16,192]{1,0:T(8,128)(4,1)S(1)} %broadcast_compare_fusion), kind=kOutput, calls=%fused_computation.3 | convolution fusion | flops 15728640 | bytes 72704 | tf_op jit(solution)/shard_map/cmf,cfz->mz/dot_general | solution.py:59
  22.6 0.6 broadcast_in_dim.25
  23.2 3.5 %all-to-all-start.1 = ((bf16[16,16,128]{2,1,0:T(8,128)(2,1)}), bf16[16,16,128]{2,1,0:T(8,128)(2,1)S(1)}, u32[]{:S(2)}, u32[]{:S(2)}) async-start(bf16[16,16,128]{2,1,0:T(8,128)(2,1)} %broadcast_in_dim.25), calls=%async_computation.1 | async-start | bytes 131072 | tf_op jit(solution)/shard_map/all_to_all | solution.py:11
  26.7 6.8 %all-to-all-done.1 = bf16[16,16,128]{2,1,0:T(8,128)(2,1)S(1)} async-done(((bf16[16,16,128]{2,1,0:T(8,128)(2,1)}), bf16[16,16,128]{2,1,0:T(8,128)(2,1)S(1)}, u32[]{:S(2)}, u32[]{:S(2)}) %all-to-all-start.1) | async-done | bytes 65568 | tf_op jit(solution)/shard_map/all_to_all | solution.py:11
  34.1 9.2 %all_to_all.25 = bf16[16,8,128]{2,1,0:T(8,128)(2,1)S(1)} all-to-all(bf16[16,8,128]{2,1,0:T(8,128)(2,1)S(1)} %broadcast_in_dim.46), channel_id=1, replica_groups=mesh['sweep'=2,'xsec'=16] {'xsec'}, dimensions={0} | all-to-all | bytes 65536 | tf_op jit(solution)/shard_map/all_to_all | solution.py:11
  43.7 0.6 broadcast_in_dim.47
  44.3 2.5 %all-to-all-start.3 = ((bf16[32,8,128]{2,1,0:T(8,128)(2,1)}), bf16[32,8,128]{2,1,0:T(8,128)(2,1)S(1)}, u32[]{:S(2)}, u32[]{:S(2)}) async-start(bf16[32,8,128]{2,1,0:T(8,128)(2,1)} %broadcast_in_dim.47), calls=%async_computation.3 | async-start | bytes 131072 | tf_op jit(solution)/shard_map/all_to_all | solution.py:11
  46.9 7.4 %all-to-all-done.3 = bf16[32,8,128]{2,1,0:T(8,128)(2,1)S(1)} async-done(((bf16[32,8,128]{2,1,0:T(8,128)(2,1)}), bf16[32,8,128]{2,1,0:T(8,128)(2,1)S(1)}, u32[]{:S(2)}, u32[]{:S(2)}) %all-to-all-start.3) | async-done | bytes 65568 | tf_op jit(solution)/shard_map/all_to_all | solution.py:11
  54.7 0.6 broadcast_in_dim.49
  55.4 3.5 %all-to-all-start.4 = ((bf16[16,8,128]{2,1,0:T(8,128)(2,1)}), bf16[16,8,128]{2,1,0:T(8,128)(2,1)S(1)}, u32[]{:S(2)}, u32[]{:S(2)}) async-start(bf16[16,8,128]{2,1,0:T(8,128)(2,1)} %broadcast_in_dim.49), calls=%async_computation.4 | async-start | bytes 65536 | tf_op jit(solution)/shard_map/all_to_all | solution.py:11
  58.8 6.6 %all-to-all-done.4 = bf16[16,8,128]{2,1,0:T(8,128)(2,1)S(1)} async-done(((bf16[16,8,128]{2,1,0:T(8,128)(2,1)}), bf16[16,8,128]{2,1,0:T(8,128)(2,1)S(1)}, u32[]{:S(2)}, u32[]{:S(2)}) %all-to-all-start.4) | async-done | bytes 32800 | tf_op jit(solution)/shard_map/all_to_all | solution.py:11
  65.8 0.6 pad_maximum_fusion.7
  (46 shorter events, 2.4 us)
Async XLA Ops:
  4.1 9.9 %copy-start.1 = (f32[2,2,128]{2,1,0:T(2,128)S(1)}, f32[2,2,128]{2,1,0:T(2,128)}, u32[]{:S(2)}) copy-start(f32[2,2,128]{2,1,0:T(2,128)} %param.10) | copy-start | bytes 6148
  4.1 10.0 %copy-start.2 = (s32[1,1,16]{2,1,0:T(1,128)S(1)}, s32[1,1,16]{2,1,0:T(1,128)}, u32[]{:S(2)}) copy-start(s32[1,1,16]{2,1,0:T(1,128)} %param.9) | copy-start | bytes 196
  4.1 16.8 %copy-start.3 = (s32[1,1,16,192]{3,2,1,0:T(8,128)S(1)}, s32[1,1,16,192]{3,2,1,0:T(8,128)}, u32[]{:S(2)}) copy-start(s32[1,1,16,192]{3,2,1,0:T(8,128)} %param.8) | copy-start | bytes 36868
  5.8 27.8 %copy-start = (bf16[2,2,2048,128]{3,2,1,0:T(8,128)(2,1)S(1)}, bf16[2,2,2048,128]{3,2,1,0:T(8,128)(2,1)}, u32[]{:S(2)}) copy-start(bf16[2,2,2048,128]{3,2,1,0:T(8,128)(2,1)} %param.11) | copy-start | bytes 6291460
  6.6 14.3 %all-to-all-start = ((bf16[16,8,192]{2,1,0:T(8,128)(2,1)}), bf16[16,8,192]{2,1,0:T(8,128)(2,1)S(1)}, u32[]{:S(2)}, u32[]{:S(2)}) async-start(bf16[16,8,192]{2,1,0:T(8,128)(2,1)} %copy.27), calls=%async_computation | async-start | bytes 131072 | tf_op jit(solution)/shard_map/all_to_all | solution.py:54
  23.2 10.4 %all-to-all-start.1 = ((bf16[16,16,128]{2,1,0:T(8,128)(2,1)}), bf16[16,16,128]{2,1,0:T(8,128)(2,1)S(1)}, u32[]{:S(2)}, u32[]{:S(2)}) async-start(bf16[16,16,128]{2,1,0:T(8,128)(2,1)} %broadcast_in_dim.25), calls=%async_computation.1 | async-start | bytes 131072 | tf_op jit(solution)/shard_map/all_to_all | solution.py:11
  44.3 10.0 %all-to-all-start.3 = ((bf16[32,8,128]{2,1,0:T(8,128)(2,1)}), bf16[32,8,128]{2,1,0:T(8,128)(2,1)S(1)}, u32[]{:S(2)}, u32[]{:S(2)}) async-start(bf16[32,8,128]{2,1,0:T(8,128)(2,1)} %broadcast_in_dim.47), calls=%async_computation.3 | async-start | bytes 131072 | tf_op jit(solution)/shard_map/all_to_all | solution.py:11
  55.4 10.1 %all-to-all-start.4 = ((bf16[16,8,128]{2,1,0:T(8,128)(2,1)}), bf16[16,8,128]{2,1,0:T(8,128)(2,1)S(1)}, u32[]{:S(2)}, u32[]{:S(2)}) async-start(bf16[16,8,128]{2,1,0:T(8,128)(2,1)} %broadcast_in_dim.49), calls=%async_computation.4 | async-start | bytes 65536 | tf_op jit(solution)/shard_map/all_to_all | solution.py:11

commit v2 on v1

v2 whole, which is shorter than its diff:
```python
import functools

import jax
import jax.numpy as jnp
from jax import lax
from jax.experimental import pallas as pl
from jax.experimental.pallas import tpu as pltpu
from jax.sharding import PartitionSpec as P

CAP = 8
LANES = 128
F32 = jnp.float32
BF16 = jnp.bfloat16


def iota(shape, axis):
    return lax.broadcasted_iota(jnp.int32, shape, axis)


def sum_sublanes(tiles):
    sub = iota((8, LANES), 0)
    low = sub < 4
    halves = [
        jnp.where(low, tiles[r], tiles[r + 4]) + pltpu.roll(jnp.where(low, tiles[r + 4], tiles[r]), 4, 0)
        for r in range(4)
    ]

    def fold(first, second, step):
        even = (sub & step) == 0
        return jnp.where(even, first, second) + jnp.where(
            even, pltpu.roll(first, 8 - step, 0), pltpu.roll(second, step, 0)
        )

    pairs = [fold(halves[r], halves[r + 2], 2) for r in range(2)]
    return fold(pairs[0], pairs[1], 1)


def swap_blocks(tiles, group):
    lane = iota((8, LANES), 1) // group
    tiles = list(tiles)
    bit = len(tiles) // 2
    while bit:
        here = (lane & bit) == 0
        for at in range(len(tiles)):
            if at & bit == 0:
                low, high = tiles[at], tiles[at + bit]
                tiles[at] = jnp.where(here, low, pltpu.roll(high, bit * group, 1))
                tiles[at + bit] = jnp.where(here, pltpu.roll(low, LANES - bit * group, 1), high)
        bit //= 2
    return tiles


def contract_kernel(cond, source, out, source32, rows):
    _, n_faces, n_inner, elems = cond.shape
    sources = source.shape[1]
    owners = LANES // CAP
    for block in range(elems // LANES):
        lanes = pl.ds(block * LANES, LANES)
        source32[...] = source[:, :, :, lanes].astype(F32)

        def one_face(face, _):
            left_re = cond[0, face, :, lanes].astype(F32)
            left_im = cond[1, face, :, lanes].astype(F32)
            tiles = [None] * (2 * sources)
            for j in range(sources):
                right_re, right_im = source32[0, j], source32[1, j]
                real = left_re * right_re - left_im * right_im
                imag = left_re * right_im + left_im * right_re
                tiles[j] = jnp.sum(real.reshape(n_inner // 8, 8, LANES), 0)
                tiles[sources + j] = jnp.sum(imag.reshape(n_inner // 8, 8, LANES), 0)
            rows[face] = sum_sublanes(tiles)
            return 0

        lax.fori_loop(0, n_faces, one_face, 0, unroll=True)
        parts = [[] for _ in range(owners)]
        at = 0
        while at < n_faces:
            size = owners
            while size > n_faces - at:
                size //= 2
            moved = swap_blocks([rows[at + face] for face in range(size)], CAP)
            for owner in range(owners):
                piece = moved[owner % size]
                skip = owner // size * size * CAP
                if skip:
                    piece = pltpu.roll(piece, LANES - skip, 1)
                parts[owner].append(piece[:, : size * CAP])
            at += size
        for owner in range(owners):
            out[block * owners + owner] = jnp.concatenate(parts[owner], 1).astype(BF16)


def assemble_kernel(received, index_rows, counts, coupling, loads, out):
    peers, rows, face_rows = received.shape
    slots = loads.shape[0] * loads.shape[2]
    width = loads.shape[2]
    position = iota((1, face_rows), 1) % CAP
    slot = iota((slots, face_rows), 0)
    total = jnp.zeros((rows, slots), F32)
    for sender in range(peers):
        index = jnp.where(position < counts[sender], index_rows[sender : sender + 1, :], -1)
        onehot = jnp.where(slot == index, 1.0, 0.0).astype(BF16)
        total += lax.dot_general(
            received[sender], onehot, (((1,), (1,)), ((), ())), preferred_element_type=F32
        )
    for layer in range(loads.shape[0]):
        loads[layer] = total[:, layer * width : (layer + 1) * width]
    couple_first = coupling[0]
    high = couple_first.astype(BF16).astype(F32)
    extra = jnp.concatenate([high, couple_first - high, jnp.zeros((4, width), F32)], 0)
    block = jnp.concatenate([total[:, :width], extra], 0).astype(BF16)
    for peer in range(out.shape[0]):
        out[peer] = block


def side_by_side(blocks):
    return jnp.concatenate(blocks, 1)


def couple(loads, coupling, carried):
    half = loads.shape[0] // 2
    couple_re, couple_im = coupling[0:1], coupling[1:2]
    real, imag = carried[:half], carried[half:]
    return jnp.concatenate(
        [
            loads[:half] - (couple_re * real - couple_im * imag),
            loads[half:] - (couple_re * imag + couple_im * real),
        ],
        0,
    )


def apply_schur(rhs, schur, layer):
    half = rhs.shape[0] // 2
    first = jnp.dot(rhs, schur[layer, 0], preferred_element_type=F32)
    second = jnp.dot(rhs, schur[layer, 1], preferred_element_type=F32)
    return jnp.concatenate([first[:half] - second[half:], second[:half] + first[half:]], 0)


def start_kernel(whole, loads, coupling, schur, out):
    count = loads.shape[1]
    rhs = side_by_side([whole[peer].astype(F32)[:count].astype(BF16) for peer in range(whole.shape[0])])
    solved = apply_schur(rhs, schur, 0)
    block = couple(loads[1], coupling[1], solved).astype(BF16)
    for peer in range(out.shape[0]):
        out[peer] = block


def next_kernel(gathered, loads, coupling, schur, out, *, layer):
    solved = apply_schur(side_by_side([gathered[peer] for peer in range(gathered.shape[0])]), schur, layer)
    block = solved.astype(BF16) if loads is None else couple(loads[layer + 1], coupling[layer + 1], solved).astype(BF16)
    for peer in range(out.shape[0]):
        out[peer] = block


def cross_kernel(everyone, whole, loads, coupling, schur, out, solved_out):
    peers = whole.shape[0]
    count = loads.shape[1]
    row = lax.axis_index("sweep")
    start = jnp.maximum(row - 1, 0) * peers
    keep = (row > 0).astype(F32)
    blocks = []
    for peer in range(peers):
        piece = whole[peer].astype(F32)
        pair = piece[count : count + 2] + piece[count + 2 : count + 4]
        before = everyone[start + peer].astype(F32) * keep
        blocks.append(couple(piece[:count], pair, before).astype(BF16))
    solved = apply_schur(side_by_side(blocks), schur, 0)
    solved_out[...] = solved
    block = couple(loads[1], coupling[1], solved).astype(BF16)
    for peer in range(out.shape[0]):
        out[peer] = block


def last_kernel(gathered, first, schur, out, *, layer):
    out[0] = first[...]
    out[layer] = apply_schur(
        side_by_side([gathered[peer] for peer in range(gathered.shape[0])]), schur, layer
    )


def call(kernel, out_shape, operands, scratch=(), scalars=()):
    specs = [
        pl.BlockSpec(memory_space=pltpu.SMEM if at in scalars else pltpu.VMEM) for at in range(len(operands))
    ]
    out_specs = jax.tree.map(lambda _: pl.BlockSpec(memory_space=pltpu.VMEM), out_shape)
    return pl.pallas_call(
        kernel,
        out_shape=out_shape,
        in_specs=specs,
        out_specs=out_specs,
        scratch_shapes=list(scratch),
        compiler_params=pltpu.CompilerParams(vmem_limit_bytes=16 * 1024 * 1024),
    )(*operands)


def exchange(blocks, axes):
    return lax.all_to_all(blocks, axes, split_axis=0, concat_axis=0, tiled=True)


def shards(cond_block, interior_src, face_index, owner_count, coupling, schur_inv):
    layers = schur_inv.shape[0]
    width = schur_inv.shape[3]
    sources = interior_src.shape[3]
    n_faces, n_inner, elems = cond_block.shape[3:]
    peers = lax.axis_size("xsec")
    chain = lax.axis_size("sweep")
    count = 2 * sources
    struct = jax.ShapeDtypeStruct

    outgoing = call(
        contract_kernel,
        struct((peers, count, n_faces * CAP), BF16),
        (cond_block[0, 0], interior_src[0, 0]),
        scratch=(pltpu.VMEM((2, sources, n_inner, LANES), F32), pltpu.VMEM((n_faces, count, LANES), F32)),
    )
    received = exchange(outgoing, "xsec")
    loads, block = call(
        assemble_kernel,
        (struct((layers, count, width), F32), struct((peers, 16, width), BF16)),
        (received, face_index[0, 0], owner_count[0, 0], coupling),
        scalars=(2,),
    )
    whole = exchange(block, "xsec")
    gathered_shape = struct((peers, count, width), BF16)
    block = call(start_kernel, gathered_shape, (whole, loads, coupling, schur_inv))
    for round_at in range(chain):
        if round_at:
            block, first = call(
                cross_kernel,
                (gathered_shape, struct((count, width), F32)),
                (everyone, whole, loads, coupling, schur_inv),
            )
        for layer in range(1, layers - 1):
            raise NotImplementedError
        gathered = exchange(block, "xsec")
        if round_at < chain - 1:
            block = call(
                functools.partial(send_kernel, layer=layers - 1),
                struct((chain * peers, count, width), BF16),
                (gathered, schur_inv),
            )
            everyone = exchange(block, ("sweep", "xsec"))
    return call(
        functools.partial(last_kernel, layer=layers - 1),
        struct((layers, count, width), F32),
        (gathered, first, schur_inv),
    )


def send_kernel(gathered, schur, out, *, layer):
    next_kernel(gathered, None, None, schur, out, layer=layer)


def solution(mesh):
    placed = (
        P("sweep", "xsec", None, None, None, None),
        P("sweep", "xsec", None, None, None, None),
        P("sweep", "xsec", None, None),
        P("sweep", "xsec", None),
        P("sweep", None, "xsec"),
        P("sweep", None, None, "xsec"),
    )
    return jax.shard_map(
        shards, mesh=mesh, in_specs=placed, out_specs=P("sweep", None, "xsec"), check_vma=False
    )
```

time: 66.9 us -> 61.7 us (0.922)
  blocking collectives: 9.2 us -> 51.2 us
  waiting for transfers between devices: 27.5 us -> 0 us
  starting transfers between devices: 16.8 us -> 0 us
  matrix products: 5.1 us -> 0 us
  Pallas kernels: 0 us -> 3.71 us
  other arithmetic: 1.17 us -> 0 us
    all_to_all x1 -> x5, blocking collectives: 9.2 us -> 51.2 us  [exchange(): return lax.all_to_all(blocks, axes, split_axis=0, concat_axis=0, tiled=True)]
    all_to_all x4 -> x0, waiting for transfers between devices: 27.5 us -> none  [the longest x3 20.8 us: spread(): return lax.all_to_all(copies, axes, split_axis=0, concat_axis=0, tiled=True)]
    all_to_all x4 -> x0, starting transfers between devices: 16.8 us -> none  [the longest x3 9.49 us: spread(): return lax.all_to_all(copies, axes, split_axis=0, concat_axis=0, tiled=True)]
    unnamed x8 -> x16, local copies, waits for them, and re-layouts: 0.02 us -> 6.24 us
    dot_general x13 -> x0, matrix products: 5.1 us -> none  [the longest x4 2.08 us: contract(): jnp.einsum('kidp,sidp->dskp', first, second, preferred_element_type=jnp.f...]
    pallas_call x0 -> x6, Pallas kernels: none -> 3.71 us  [call(): pl.pallas_call(kernel, out_shape=out_shape, in_specs=specs, out_specs=out...]
    slice x9 -> x0, local copies, waits for them, and re-layouts: 3.06 us -> none  [the longest x2 1.53 us: shards(): couple_blocks[1]]
    broadcast_in_dim x5 -> x0, local copies, waits for them, and re-layouts: 1.91 us -> none  [the longest x4 1.91 us: spread(): copies = jnp.broadcast_to(block[None], (count,) + block.shape)]
  transfers between devices with their start and end apart: 4 -> 0, of which waited for: 4 -> 0; matrix products, arithmetic and copies ran while one was open for 0% -> 0% of each run, Pallas kernels for 0% -> 0%
where the time goes in v2:
time: 61.7 us; the launch traced here: 61.2 us
  blocking collectives  51.2 us (83%)
  local copies, waits for them, and re-layouts  6.24 us (10%)
  Pallas kernels  3.71 us (6%)
    all_to_all x5, blocking collectives, exchange(): return lax.all_to_all(blocks, axes, split_axis=0, concat_axis=0, tiled=True)  51.2 us
    unnamed x16, local copies, waits for them, and re-layouts  6.24 us
    pallas_call x6, Pallas kernels, call(): pl.pallas_call(kernel, out_shape=out_shape, in_specs=specs, out_specs=out...  3.71 us

profile of v2, /device:TPU:0, one launch (start us, length us, event | category | flops | bytes accessed | tf_op | source)
XLA Modules:
  0.0 61.2 jit_solution(405800437289255408)
XLA Ops:
  0.0 1.0 %copy-done.2 = bf16[1,1,2,24,40,128]{5,4,3,2,1,0:T(8,128)(2,1)S(1)} copy-done((bf16[1,1,2,24,40,128]{5,4,3,2,1,0:T(8,128)(2,1)S(1)}, bf16[1,1,2,24,40,128]{5,4,3,2,1,0:T(8,128)(2,1)}, u32[]{:S(2)}) %copy-start.2) | copy-done | bytes 491544
  1.0 0.0 copy-start.3
  1.0 0.9 %copy-done.3 = bf16[1,1,2,4,40,128]{5,4,3,2,1,0:T(8,128)(2,1)S(1)} copy-done((bf16[1,1,2,4,40,128]{5,4,3,2,1,0:T(8,128)(2,1)S(1)}, bf16[1,1,2,4,40,128]{5,4,3,2,1,0:T(8,128)(2,1)}, u32[]{:S(2)}) %copy-start.3) | copy-done | bytes 81944
  1.9 0.9 %shard_map.64 = bf16[16,8,192]{2,1,0:T(8,128)(2,1)S(1)} custom-call(bf16[2,24,40,128]{3,2,1,0:T(8,128)(2,1)S(1)} %bitcast.4, bf16[2,4,40,128]{3,2,1,0:T(8,128)(2,1)S(1)} %bitcast.5), custom_call_target="tpu_custom_call" | custom-call | tf_op jit(solution)/shard_map/pallas_call | solution.py:187
  2.8 14.0 %all_to_all.25.received = bf16[16,8,192]{2,1,0:T(8,128)(2,1)S(1)} all-to-all(bf16[16,8,192]{2,1,0:T(8,128)(2,1)S(1)} %shard_map.64), channel_id=1, replica_groups=mesh['sweep'=2,'xsec'=16] {'xsec'}, dimensions={0} | all-to-all | bytes 98304 | tf_op jit(solution)/shard_map/all_to_all | solution.py:198
  16.9 0.0 copy-start.4
  16.9 0.7 %copy-done.4 = f32[2,2,128]{2,1,0:T(2,128)S(1)} copy-done((f32[2,2,128]{2,1,0:T(2,128)S(1)}, f32[2,2,128]{2,1,0:T(2,128)}, u32[]{:S(2)}) %copy-start.4) | copy-done | bytes 2072
  17.6 0.0 copy-start.6
  17.6 0.7 %copy-done.6 = s32[1,1,16,192]{3,2,1,0:T(8,128)S(1)} copy-done((s32[1,1,16,192]{3,2,1,0:T(8,128)S(1)}, s32[1,1,16,192]{3,2,1,0:T(8,128)}, u32[]{:S(2)}) %copy-start.6) | copy-done | bytes 12312
  18.3 0.0 copy-start.7
  18.3 0.7 %copy-done.7 = s32[1,1,16]{2,1,0:T(1,128)S(1)} copy-done((s32[1,1,16]{2,1,0:T(1,128)S(1)}, s32[1,1,16]{2,1,0:T(1,128)}, u32[]{:S(2)}) %copy-start.7) | copy-done | bytes 88
  18.9 1.2 %shard_map.65 = (f32[2,8,128]{2,1,0:T(8,128)S(1)}, bf16[16,16,128]{2,1,0:T(8,128)(2,1)S(1)}) custom-call(bf16[16,8,192]{2,1,0:T(8,128)(2,1)S(1)} %all_to_all.25.received, s32[16,192]{1,0:T(8,128)S(1)} %bitcast.6, s32[16]{0:T(128)S(1)} %bitcast.7, f32[2,2,128]{2,1,0:T(2,128)S(1)} %copy-done.4), custom_call_target="tpu_custom_call" | custom-call | tf_op jit(solution)/shard_map/pallas_call | solution.py:187
  20.1 9.5 %all_to_all.26.whole = bf16[16,16,128]{2,1,0:T(8,128)(2,1)S(1)} all-to-all(bf16[16,16,128]{2,1,0:T(8,128)(2,1)S(1)} %get-tuple-element.9), channel_id=1, replica_groups=mesh['sweep'=2,'xsec'=16] {'xsec'}, dimensions={0} | all-to-all | bytes 131072 | tf_op jit(solution)/shard_map/all_to_all | solution.py:198
  29.6 0.0 copy-start
  29.6 1.6 %copy-done = bf16[2,2,2048,128]{3,2,1,0:T(8,128)(2,1)S(1)} copy-done((bf16[2,2,2048,128]{3,2,1,0:T(8,128)(2,1)S(1)}, bf16[2,2,2048,128]{3,2,1,0:T(8,128)(2,1)}, u32[]{:S(2)}) %copy-start) | copy-done | bytes 2097176
  31.2 0.7 %copy-done.5 = f32[2,2,128]{2,1,0:T(2,128)S(1)} copy-done((f32[2,2,128]{2,1,0:T(2,128)S(1)}, f32[2,2,128]{2,1,0:T(2,128)}, u32[]{:S(2)}) %copy-start.5) | copy-done | bytes 2072
  31.9 0.3 shard_map.66
  32.1 9.3 %all_to_all.27.gathered = bf16[16,8,128]{2,1,0:T(8,128)(2,1)S(1)} all-to-all(bf16[16,8,128]{2,1,0:T(8,128)(2,1)S(1)} %shard_map.66), channel_id=1, replica_groups=mesh['sweep'=2,'xsec'=16] {'xsec'}, dimensions={0} | all-to-all | bytes 65536 | tf_op jit(solution)/shard_map/all_to_all | solution.py:198
  41.5 0.0 copy-done.1
  41.5 0.2 shard_map.67
  41.7 9.1 %all_to_all.28.everyone = bf16[32,8,128]{2,1,0:T(8,128)(2,1)S(1)} all-to-all(bf16[32,8,128]{2,1,0:T(8,128)(2,1)S(1)} %shard_map.67), channel_id=1, replica_groups=mesh['sweep'=2,'xsec'=16] {'sweep','xsec'}, dimensions={0} | all-to-all | bytes 131072 | tf_op jit(solution)/shard_map/all_to_all | solution.py:198
  50.8 0.3 shard_map.68
  51.1 9.2 %all_to_all.29.gathered = bf16[16,8,128]{2,1,0:T(8,128)(2,1)S(1)} all-to-all(bf16[16,8,128]{2,1,0:T(8,128)(2,1)S(1)} %get-tuple-element.11), channel_id=1, replica_groups=mesh['sweep'=2,'xsec'=16] {'xsec'}, dimensions={0} | all-to-all | bytes 65536 | tf_op jit(solution)/shard_map/all_to_all | solution.py:198
  60.3 0.9 %shard_map.69 = f32[2,8,128]{2,1,0:T(8,128)} custom-call(bf16[16,8,128]{2,1,0:T(8,128)(2,1)S(1)} %all_to_all.29.gathered, f32[8,128]{1,0:T(8,128)S(1)} %get-tuple-element.12.first, bf16[2,2,2048,128]{3,2,1,0:T(8,128)(2,1)S(1)} %copy-done.1), custom_call_target="tpu_custom_call" | custom-call | tf_op jit(solution)/shard_map/pallas_call | solution.py:187
  (3 shorter events, 0.0 us)
Async XLA Ops:
  0.0 1.0 %copy-start.2 = (bf16[1,1,2,24,40,128]{5,4,3,2,1,0:T(8,128)(2,1)S(1)}, bf16[1,1,2,24,40,128]{5,4,3,2,1,0:T(8,128)(2,1)}, u32[]{:S(2)}) copy-start(bf16[1,1,2,24,40,128]{5,4,3,2,1,0:T(8,128)(2,1)} %param.6) | copy-start | bytes 1474564
  1.0 0.9 %copy-start.3 = (bf16[1,1,2,4,40,128]{5,4,3,2,1,0:T(8,128)(2,1)S(1)}, bf16[1,1,2,4,40,128]{5,4,3,2,1,0:T(8,128)(2,1)}, u32[]{:S(2)}) copy-start(bf16[1,1,2,4,40,128]{5,4,3,2,1,0:T(8,128)(2,1)} %param.7) | copy-start | bytes 245764
  16.9 0.7 %copy-start.4 = (f32[2,2,128]{2,1,0:T(2,128)S(1)}, f32[2,2,128]{2,1,0:T(2,128)}, u32[]{:S(2)}) copy-start(f32[2,2,128]{2,1,0:T(2,128)} %coupling.5) | copy-start | bytes 6148
  17.6 0.7 %copy-start.6 = (s32[1,1,16,192]{3,2,1,0:T(8,128)S(1)}, s32[1,1,16,192]{3,2,1,0:T(8,128)}, u32[]{:S(2)}) copy-start(s32[1,1,16,192]{3,2,1,0:T(8,128)} %param.8) | copy-start | bytes 36868
  18.3 0.7 %copy-start.7 = (s32[1,1,16]{2,1,0:T(1,128)S(1)}, s32[1,1,16]{2,1,0:T(1,128)}, u32[]{:S(2)}) copy-start(s32[1,1,16]{2,1,0:T(1,128)} %param.9) | copy-start | bytes 196
  29.6 1.6 %copy-start = (bf16[2,2,2048,128]{3,2,1,0:T(8,128)(2,1)S(1)}, bf16[2,2,2048,128]{3,2,1,0:T(8,128)(2,1)}, u32[]{:S(2)}) copy-start(bf16[2,2,2048,128]{3,2,1,0:T(8,128)(2,1)} %schur.7) | copy-start | bytes 6291460
  31.2 0.7 %copy-start.5 = (f32[2,2,128]{2,1,0:T(2,128)S(1)}, f32[2,2,128]{2,1,0:T(2,128)}, u32[]{:S(2)}) copy-start(f32[2,2,128]{2,1,0:T(2,128)} %coupling.5) | copy-start | bytes 6148
  31.9 9.6 %copy-start.1 = (bf16[2,2,2048,128]{3,2,1,0:T(8,128)(2,1)S(1)}, bf16[2,2,2048,128]{3,2,1,0:T(8,128)(2,1)}, u32[]{:S(2)}) copy-start(bf16[2,2,2048,128]{3,2,1,0:T(8,128)(2,1)} %schur.7) | copy-start | bytes 6291460

commit v3 on v2

--- a/solution.py
+++ b/solution.py
@@ -9,6 +9,7 @@
 
 CAP = 8
 LANES = 128
+CHUNKS = 4
 F32 = jnp.float32
 BF16 = jnp.bfloat16
 
@@ -50,28 +51,47 @@
     return tiles
 
 
-def contract_kernel(cond, source, out, source32, rows):
+def contract_kernel(
+    cond_hbm, source_hbm, index_hbm, counts_hbm, coupling_hbm, schur_hbm,
+    out, index_out, coupling_out, schur_out,
+    cond, source, index_rows, counts, source32, rows, sems,
+):
     _, n_faces, n_inner, elems = cond.shape
     sources = source.shape[1]
     owners = LANES // CAP
+    faces_each = n_faces // CHUNKS
+    copies = [pltpu.make_async_copy(source_hbm, source, sems.at[0])]
+    for chunk in range(CHUNKS):
+        some = pl.ds(chunk * faces_each, faces_each)
+        copies.append(pltpu.make_async_copy(cond_hbm.at[:, some], cond.at[:, some], sems.at[1 + chunk]))
+    rest = [
+        pltpu.make_async_copy(index_hbm, index_rows, sems.at[1 + CHUNKS]),
+        pltpu.make_async_copy(counts_hbm, counts, sems.at[2 + CHUNKS]),
+        pltpu.make_async_copy(coupling_hbm, coupling_out, sems.at[3 + CHUNKS]),
+        pltpu.make_async_copy(schur_hbm, schur_out, sems.at[4 + CHUNKS]),
+    ]
+    for copy in copies + rest:
+        copy.start()
+    copies[0].wait()
     for block in range(elems // LANES):
         lanes = pl.ds(block * LANES, LANES)
-        source32[...] = source[:, :, :, lanes].astype(F32)
-
-        def one_face(face, _):
+        source32[:2] = source[:, :, :, lanes].astype(F32)
+        source32[2] = source32[0] + source32[1]
+        for face in range(n_faces):
+            if block == 0 and face % faces_each == 0:
+                copies[1 + face // faces_each].wait()
             left_re = cond[0, face, :, lanes].astype(F32)
             left_im = cond[1, face, :, lanes].astype(F32)
+            left_sum = left_re + left_im
+            left_gap = left_im - left_re
             tiles = [None] * (2 * sources)
             for j in range(sources):
-                right_re, right_im = source32[0, j], source32[1, j]
-                real = left_re * right_re - left_im * right_im
-                imag = left_re * right_im + left_im * right_re
-                tiles[j] = jnp.sum(real.reshape(n_inner // 8, 8, LANES), 0)
-                tiles[sources + j] = jnp.sum(imag.reshape(n_inner // 8, 8, LANES), 0)
+                both = jnp.sum((left_re * source32[2, j]).reshape(n_inner // 8, 8, LANES), 0)
+                minus = jnp.sum((left_sum * source32[1, j]).reshape(n_inner // 8, 8, LANES), 0)
+                plus = jnp.sum((left_gap * source32[0, j]).reshape(n_inner // 8, 8, LANES), 0)
+                tiles[j] = both - minus
+                tiles[sources + j] = both + plus
             rows[face] = sum_sublanes(tiles)
-            return 0
-
-        lax.fori_loop(0, n_faces, one_face, 0, unroll=True)
         parts = [[] for _ in range(owners)]
         at = 0
         while at < n_faces:
@@ -88,18 +108,22 @@
             at += size
         for owner in range(owners):
             out[block * owners + owner] = jnp.concatenate(parts[owner], 1).astype(BF16)
-
-
-def assemble_kernel(received, index_rows, counts, coupling, loads, out):
+    for copy in rest:
+        copy.wait()
+    position = iota((1, index_rows.shape[1]), 1) % CAP
+    for sender in range(index_rows.shape[0]):
+        row = index_rows[sender : sender + 1, :]
+        index_out[sender : sender + 1, :] = jnp.where(position < counts[sender], row, -1)
+
+
+def assemble_kernel(received, index_rows, coupling, loads, out):
     peers, rows, face_rows = received.shape
     slots = loads.shape[0] * loads.shape[2]
     width = loads.shape[2]
-    position = iota((1, face_rows), 1) % CAP
     slot = iota((slots, face_rows), 0)
     total = jnp.zeros((rows, slots), F32)
     for sender in range(peers):
-        index = jnp.where(position < counts[sender], index_rows[sender : sender + 1, :], -1)
-        onehot = jnp.where(slot == index, 1.0, 0.0).astype(BF16)
+        onehot = jnp.where(slot == index_rows[sender : sender + 1, :], 1.0, 0.0).astype(BF16)
         total += lax.dot_general(
             received[sender], onehot, (((1,), (1,)), ((), ())), preferred_element_type=F32
         )
@@ -179,16 +203,14 @@
     )
 
 
-def call(kernel, out_shape, operands, scratch=(), scalars=()):
-    specs = [
-        pl.BlockSpec(memory_space=pltpu.SMEM if at in scalars else pltpu.VMEM) for at in range(len(operands))
-    ]
-    out_specs = jax.tree.map(lambda _: pl.BlockSpec(memory_space=pltpu.VMEM), out_shape)
+def call(kernel, out_shape, operands, scratch=(), space=pltpu.VMEM):
+    if space == pltpu.HBM:
+        operands = [pltpu.with_memory_space_constraint(operand, space) for operand in operands]
     return pl.pallas_call(
         kernel,
         out_shape=out_shape,
-        in_specs=specs,
-        out_specs=out_specs,
+        in_specs=[pl.BlockSpec(memory_space=space)] * len(operands),
+        out_specs=jax.tree.map(lambda _: pl.BlockSpec(memory_space=pltpu.VMEM), out_shape),
         scratch_shapes=list(scratch),
         compiler_params=pltpu.CompilerParams(vmem_limit_bytes=16 * 1024 * 1024),
     )(*operands)
@@ -208,18 +230,32 @@
     count = 2 * sources
     struct = jax.ShapeDtypeStruct
 
-    outgoing = call(
+    index_rows = face_index[0, 0]
+    outgoing, index_rows, coupling, schur_inv = call(
         contract_kernel,
-        struct((peers, count, n_faces * CAP), BF16),
-        (cond_block[0, 0], interior_src[0, 0]),
-        scratch=(pltpu.VMEM((2, sources, n_inner, LANES), F32), pltpu.VMEM((n_faces, count, LANES), F32)),
+        (
+            struct((peers, count, n_faces * CAP), BF16),
+            struct(index_rows.shape, index_rows.dtype),
+            struct(coupling.shape, coupling.dtype),
+            struct(schur_inv.shape, schur_inv.dtype),
+        ),
+        (cond_block[0, 0], interior_src[0, 0], index_rows, owner_count[0, 0], coupling, schur_inv),
+        scratch=(
+            pltpu.VMEM(cond_block.shape[2:], BF16),
+            pltpu.VMEM(interior_src.shape[2:], BF16),
+            pltpu.VMEM(index_rows.shape, index_rows.dtype),
+            pltpu.SMEM(owner_count.shape[2:], owner_count.dtype),
+            pltpu.VMEM((3, sources, n_inner, LANES), F32),
+            pltpu.VMEM((n_faces, count, LANES), F32),
+            pltpu.SemaphoreType.DMA((5 + CHUNKS,)),
+        ),
+        space=pltpu.HBM,
     )
     received = exchange(outgoing, "xsec")
     loads, block = call(
         assemble_kernel,
         (struct((layers, count, width), F32), struct((peers, 16, width), BF16)),
-        (received, face_index[0, 0], owner_count[0, 0], coupling),
-        scalars=(2,),
+        (received, index_rows, coupling),
     )
     whole = exchange(block, "xsec")
     gathered_shape = struct((peers, count, width), BF16)

time: 61.7 us -> 55.7 us (0.903)
  local copies, waits for them, and re-layouts: 6.24 us -> 0 us
    unnamed x16 -> x0, local copies, waits for them, and re-layouts: 6.24 us -> none
where the time goes in v3:
time: 55.7 us; the launch traced here: 55.4 us
  blocking collectives  51.1 us (92%)
  Pallas kernels  4.3 us (8%)
    all_to_all x5, blocking collectives, exchange(): return lax.all_to_all(blocks, axes, split_axis=0, concat_axis=0, tiled=True)  51.1 us
    pallas_call x6, Pallas kernels, call(): pl.pallas_call(kernel, out_shape=out_shape, in_specs=[pl.BlockSpec(memory...  4.3 us

profile of v3, /device:TPU:0, one launch (start us, length us, event | category | flops | bytes accessed | tf_op | source)
XLA Modules:
  0.0 55.4 jit_solution(18146575840572283097)
XLA Ops:
  0.0 2.0 %shard_map.64 = (bf16[16,8,192]{2,1,0:T(8,128)(2,1)S(1)}, s32[16,192]{1,0:T(8,128)S(1)}, f32[2,2,128]{2,1,0:T(2,128)S(1)}, bf16[2,2,2048,128]{3,2,1,0:T(8,128)(2,1)S(1)}) custom-call(bf16[2,24,40,128]{3,2,1,0:T(8,128)(2,1)} %bitcast.4, bf16[2,4,40,128]{3,2,1,0:T(8,128)(2,1)} %bitcast.5, s32[16,192]{1,0:T(8,128)} %bitcast.6, s32[16]{0:T(128)} %bitcast.7, ...), custom_call_target="tpu_custom_call" | custom-call | tf_op jit(solution)/shard_map/pallas_call | solution.py:209
  2.0 14.1 %all_to_all.25.received = bf16[16,8,192]{2,1,0:T(8,128)(2,1)S(1)} all-to-all(bf16[16,8,192]{2,1,0:T(8,128)(2,1)S(1)} %get-tuple-element.13), channel_id=1, replica_groups=mesh['sweep'=2,'xsec'=16] {'xsec'}, dimensions={0} | all-to-all | bytes 98304 | tf_op jit(solution)/shard_map/all_to_all | solution.py:220
  16.1 0.6 %shard_map.65 = (f32[2,8,128]{2,1,0:T(8,128)S(1)}, bf16[16,16,128]{2,1,0:T(8,128)(2,1)S(1)}) custom-call(bf16[16,8,192]{2,1,0:T(8,128)(2,1)S(1)} %all_to_all.25.received, s32[16,192]{1,0:T(8,128)S(1)} %get-tuple-element.14.index_rows, f32[2,2,128]{2,1,0:T(2,128)S(1)} %get-tuple-element.15.coupling), custom_call_target="tpu_custom_call" | custom-call | tf_op jit(solution)/shard_map/pallas_call | solution.py:209
  16.7 9.5 %all_to_all.26.whole = bf16[16,16,128]{2,1,0:T(8,128)(2,1)S(1)} all-to-all(bf16[16,16,128]{2,1,0:T(8,128)(2,1)S(1)} %get-tuple-element.16), channel_id=1, replica_groups=mesh['sweep'=2,'xsec'=16] {'xsec'}, dimensions={0} | all-to-all | bytes 131072 | tf_op jit(solution)/shard_map/all_to_all | solution.py:220
  26.2 0.3 shard_map.66
  26.5 9.2 %all_to_all.27.gathered = bf16[16,8,128]{2,1,0:T(8,128)(2,1)S(1)} all-to-all(bf16[16,8,128]{2,1,0:T(8,128)(2,1)S(1)} %shard_map.66), channel_id=1, replica_groups=mesh['sweep'=2,'xsec'=16] {'xsec'}, dimensions={0} | all-to-all | bytes 65536 | tf_op jit(solution)/shard_map/all_to_all | solution.py:220
  35.7 0.2 shard_map.67
  36.0 9.1 %all_to_all.28.everyone = bf16[32,8,128]{2,1,0:T(8,128)(2,1)S(1)} all-to-all(bf16[32,8,128]{2,1,0:T(8,128)(2,1)S(1)} %shard_map.67), channel_id=1, replica_groups=mesh['sweep'=2,'xsec'=16] {'sweep','xsec'}, dimensions={0} | all-to-all | bytes 131072 | tf_op jit(solution)/shard_map/all_to_all | solution.py:220
  45.1 0.3 shard_map.68
  45.3 9.2 %all_to_all.29.gathered = bf16[16,8,128]{2,1,0:T(8,128)(2,1)S(1)} all-to-all(bf16[16,8,128]{2,1,0:T(8,128)(2,1)S(1)} %get-tuple-element.19), channel_id=1, replica_groups=mesh['sweep'=2,'xsec'=16] {'xsec'}, dimensions={0} | all-to-all | bytes 65536 | tf_op jit(solution)/shard_map/all_to_all | solution.py:220
  54.5 0.9 %shard_map.69 = f32[2,8,128]{2,1,0:T(8,128)} custom-call(bf16[16,8,128]{2,1,0:T(8,128)(2,1)S(1)} %all_to_all.29.gathered, f32[8,128]{1,0:T(8,128)S(1)} %get-tuple-element.20.first, bf16[2,2,2048,128]{3,2,1,0:T(8,128)(2,1)S(1)} %get-tuple-element.18.schur), custom_call_target="tpu_custom_call" | custom-call | tf_op jit(solution)/shard_map/pallas_call | solution.py:209

commit v4 on v3

--- a/solution.py
+++ b/solution.py
@@ -161,46 +161,54 @@
     return jnp.concatenate([first[:half] - second[half:], second[:half] + first[half:]], 0)
 
 
-def start_kernel(whole, loads, coupling, schur, out):
-    count = loads.shape[1]
-    rhs = side_by_side([whole[peer].astype(F32)[:count].astype(BF16) for peer in range(whole.shape[0])])
-    solved = apply_schur(rhs, schur, 0)
-    block = couple(loads[1], coupling[1], solved).astype(BF16)
-    for peer in range(out.shape[0]):
-        out[peer] = block
-
-
-def next_kernel(gathered, loads, coupling, schur, out, *, layer):
-    solved = apply_schur(side_by_side([gathered[peer] for peer in range(gathered.shape[0])]), schur, layer)
-    block = solved.astype(BF16) if loads is None else couple(loads[layer + 1], coupling[layer + 1], solved).astype(BF16)
-    for peer in range(out.shape[0]):
-        out[peer] = block
-
-
-def cross_kernel(everyone, whole, loads, coupling, schur, out, solved_out):
+def round_kernel(*refs, row_at):
+    if row_at is None:
+        whole, loads, coupling, schur, out, solved_out = refs
+    else:
+        everyone, whole, loads, coupling, schur, out, solved_out = refs
     peers = whole.shape[0]
     count = loads.shape[1]
-    row = lax.axis_index("sweep")
-    start = jnp.maximum(row - 1, 0) * peers
-    keep = (row > 0).astype(F32)
+    if row_at is not None:
+        row = lax.axis_index(row_at)
+        start = jnp.maximum(row - 1, 0) * peers
+        keep = (row > 0).astype(F32)
     blocks = []
     for peer in range(peers):
         piece = whole[peer].astype(F32)
         pair = piece[count : count + 2] + piece[count + 2 : count + 4]
-        before = everyone[start + peer].astype(F32) * keep
+        if row_at is None:
+            before = jnp.zeros((count, piece.shape[1]), F32)
+        else:
+            before = everyone[start + peer].astype(F32) * keep
         blocks.append(couple(piece[:count], pair, before).astype(BF16))
-    solved = apply_schur(side_by_side(blocks), schur, 0)
+    solved = apply_schur(jnp.concatenate(blocks, 1), schur, 0)
     solved_out[...] = solved
     block = couple(loads[1], coupling[1], solved).astype(BF16)
     for peer in range(out.shape[0]):
         out[peer] = block
 
 
-def last_kernel(gathered, first, schur, out, *, layer):
-    out[0] = first[...]
-    out[layer] = apply_schur(
-        side_by_side([gathered[peer] for peer in range(gathered.shape[0])]), schur, layer
-    )
+def layer_kernel(gathered, loads, coupling, schur, out, solved_out, *, layer):
+    rhs = jnp.concatenate([gathered[peer] for peer in range(gathered.shape[0])], 1)
+    solved = apply_schur(rhs, schur, layer)
+    solved_out[...] = solved
+    block = couple(loads[layer + 1], coupling[layer + 1], solved).astype(BF16)
+    for peer in range(out.shape[0]):
+        out[peer] = block
+
+
+def last_kernel(*refs, layer, send):
+    gathered, *earlier, schur = refs[: layer + 2]
+    outs = refs[layer + 2 :]
+    rhs = jnp.concatenate([gathered[peer] for peer in range(gathered.shape[0])], 1)
+    solved = apply_schur(rhs, schur, layer)
+    for at in range(layer):
+        outs[0][at] = earlier[at][...]
+    outs[0][layer] = solved
+    if send:
+        block = solved.astype(BF16)
+        for peer in range(outs[1].shape[0]):
+            outs[1][peer] = block
 
 
 def call(kernel, out_shape, operands, scratch=(), space=pltpu.VMEM):
@@ -259,33 +267,43 @@
     )
     whole = exchange(block, "xsec")
     gathered_shape = struct((peers, count, width), BF16)
-    block = call(start_kernel, gathered_shape, (whole, loads, coupling, schur_inv))
-    for round_at in range(chain):
-        if round_at:
-            block, first = call(
-                cross_kernel,
-                (gathered_shape, struct((count, width), F32)),
-                (everyone, whole, loads, coupling, schur_inv),
+    solved_shape = struct((count, width), F32)
+    whole_out = struct((layers, count, width), F32)
+
+    def solve_round(everyone, whole, loads, coupling, schur_inv, send):
+        behind = () if everyone is None else (everyone,)
+        block, solved = call(
+            functools.partial(round_kernel, row_at="sweep" if behind else None),
+            (gathered_shape, solved_shape),
+            behind + (whole, loads, coupling, schur_inv),
+        )
+        done = [solved]
+        for layer in range(1, layers - 1):
+            block, solved = call(
+                functools.partial(layer_kernel, layer=layer),
+                (gathered_shape, solved_shape),
+                (exchange(block, "xsec"), loads, coupling, schur_inv),
             )
-        for layer in range(1, layers - 1):
-            raise NotImplementedError
-        gathered = exchange(block, "xsec")
-        if round_at < chain - 1:
-            block = call(
-                functools.partial(send_kernel, layer=layers - 1),
-                struct((chain * peers, count, width), BF16),
-                (gathered, schur_inv),
-            )
-            everyone = exchange(block, ("sweep", "xsec"))
-    return call(
-        functools.partial(last_kernel, layer=layers - 1),
-        struct((layers, count, width), F32),
-        (gathered, first, schur_inv),
-    )
-
-
-def send_kernel(gathered, schur, out, *, layer):
-    next_kernel(gathered, None, None, schur, out, layer=layer)
+            done.append(solved)
+        sent = (struct((chain * peers, count, width), BF16),) if send else ()
+        return call(
+            functools.partial(last_kernel, layer=layers - 1, send=send),
+            (whole_out,) + sent,
+            (exchange(block, "xsec"), *done, schur_inv),
+        )
+
+    everyone = solved = None
+    for round_at in range(chain - 1):
+        solved, block = solve_round(everyone, whole, loads, coupling, schur_inv, True)
+        everyone = exchange(block, ("sweep", "xsec"))
+    if chain == 1:
+        return solve_round(None, whole, loads, coupling, schur_inv, False)[0]
+    return lax.cond(
+        lax.axis_index("sweep") == chain - 1,
+        lambda solved, *rest: solve_round(*rest, False)[0],
+        lambda solved, *rest: solved,
+        solved, everyone, whole, loads, coupling, schur_inv,
+    )
 
 
 def solution(mesh):

time: 55.7 us -> 54.9 us (0.986)
  the two profiles are of different devices: /device:TPU:0 before, /device:TPU:4 now
where the time goes in v4:
time: 54.9 us; the launch traced here: 54.6 us
  blocking collectives  40.5 us (74%)
  waiting for transfers between devices  6.42 us (12%)
  Pallas kernels  4.31 us (8%)
  starting transfers between devices  2.67 us (5%)
  local copies, waits for them, and re-layouts  0.61 us (1%)
    all_to_all x4, blocking collectives, exchange(): return lax.all_to_all(blocks, axes, split_axis=0, concat_axis=0, tiled=True)  40.5 us
    all_to_all x1, waiting for transfers between devices, exchange(): return lax.all_to_all(blocks, axes, split_axis=0, concat_axis=0, tiled=True)  6.42 us
    pallas_call x6, Pallas kernels, call(): pl.pallas_call(kernel, out_shape=out_shape, in_specs=[pl.BlockSpec(memory...  4.31 us
    all_to_all x1, starting transfers between devices, exchange(): return lax.all_to_all(blocks, axes, split_axis=0, concat_axis=0, tiled=True)  2.67 us
  transfers between devices with their start and end apart: 1, of which 1 were waited for; matrix products, arithmetic and copies ran while one was open for 0% of the time, Pallas kernels for 0%

profile of v4, /device:TPU:4, one launch (start us, length us, event | category | flops | bytes accessed | tf_op | source)
XLA Modules:
  0.0 54.6 jit_solution(11290751108477452794)
XLA Ops:
  0.0 2.0 %shard_map.66 = (bf16[16,8,192]{2,1,0:T(8,128)(2,1)S(1)}, s32[16,192]{1,0:T(8,128)S(1)}, f32[2,2,128]{2,1,0:T(2,128)S(1)}, bf16[2,2,2048,128]{3,2,1,0:T(8,128)(2,1)S(1)}) custom-call(bf16[2,24,40,128]{3,2,1,0:T(8,128)(2,1)} %bitcast.4, bf16[2,4,40,128]{3,2,1,0:T(8,128)(2,1)} %bitcast.5, s32[16,192]{1,0:T(8,128)} %bitcast.6, s32[16]{0:T(128)} %bitcast.7, ...), custom_call_target="tpu_custom_call" | custom-call | tf_op jit(solution)/shard_map/pallas_call | solution.py:217
  2.0 12.6 %all_to_all.25.received = bf16[16,8,192]{2,1,0:T(8,128)(2,1)S(1)} all-to-all(bf16[16,8,192]{2,1,0:T(8,128)(2,1)S(1)} %get-tuple-element.36), channel_id=1, replica_groups=mesh['sweep'=2,'xsec'=16] {'xsec'}, dimensions={0} | all-to-all | bytes 98304 | tf_op jit(solution)/shard_map/all_to_all | solution.py:228
  14.6 0.6 %shard_map.67 = (f32[2,8,128]{2,1,0:T(8,128)S(1)}, bf16[16,16,128]{2,1,0:T(8,128)(2,1)S(1)}) custom-call(bf16[16,8,192]{2,1,0:T(8,128)(2,1)S(1)} %all_to_all.25.received, s32[16,192]{1,0:T(8,128)S(1)} %get-tuple-element.37.index_rows, f32[2,2,128]{2,1,0:T(2,128)S(1)} %get-tuple-element.38.coupling.refs_2_), custom_call_target="tpu_custom_call" | custom-call | tf_op jit(solution)/shard_map/pallas_call | solution.py:217
  15.3 9.5 %all_to_all.26.refs_0_ = bf16[16,16,128]{2,1,0:T(8,128)(2,1)S(1)} all-to-all(bf16[16,16,128]{2,1,0:T(8,128)(2,1)S(1)} %get-tuple-element.39), channel_id=1, replica_groups=mesh['sweep'=2,'xsec'=16] {'xsec'}, dimensions={0} | all-to-all | bytes 131072 | tf_op jit(solution)/shard_map/all_to_all | solution.py:228
  24.8 0.3 shard_map.68
  25.0 9.2 %all_to_all.27.refs_0_ = bf16[16,8,128]{2,1,0:T(8,128)(2,1)S(1)} all-to-all(bf16[16,8,128]{2,1,0:T(8,128)(2,1)S(1)} %get-tuple-element.42), channel_id=1, replica_groups=mesh['sweep'=2,'xsec'=16] {'xsec'}, dimensions={0} | all-to-all | bytes 65536 | tf_op jit(solution)/shard_map/all_to_all | solution.py:228
  34.2 0.9 %shard_map.69 = (f32[2,8,128]{2,1,0:T(8,128)S(1)}, bf16[32,8,128]{2,1,0:T(8,128)(2,1)}) custom-call(bf16[16,8,128]{2,1,0:T(8,128)(2,1)S(1)} %all_to_all.27.refs_0_, f32[8,128]{1,0:T(8,128)S(1)} %get-tuple-element.43.refs_1_, bf16[2,2,2048,128]{3,2,1,0:T(8,128)(2,1)S(1)} %get-tuple-element.41.refs_3_.refs_2_), custom_call_target="tpu_custom_call" | custom-call | tf_op jit(solution)/shard_map/pallas_call | solution.py:217
  35.1 2.7 %all-to-all-start.4 = ((bf16[32,8,128]{2,1,0:T(8,128)(2,1)}), bf16[32,8,128]{2,1,0:T(8,128)(2,1)S(1)}, u32[]{:S(2)}, u32[]{:S(2)}) async-start(bf16[32,8,128]{2,1,0:T(8,128)(2,1)} %get-tuple-element.45), calls=%async_computation.4 | async-start | bytes 131072 | tf_op jit(solution)/shard_map/all_to_all | solution.py:228
  37.8 6.4 %all-to-all-done.4 = bf16[32,8,128]{2,1,0:T(8,128)(2,1)S(1)} async-done(((bf16[32,8,128]{2,1,0:T(8,128)(2,1)}), bf16[32,8,128]{2,1,0:T(8,128)(2,1)S(1)}, u32[]{:S(2)}, u32[]{:S(2)}) %all-to-all-start.4) | async-done | bytes 65568 | tf_op jit(solution)/shard_map/all_to_all | solution.py:228
  44.2 9.7 %conditional.1 = (f32[2,8,128]{2,1,0:T(8,128)S(1)}) conditional(s32[]{:T(128)} %convert_element_type.3, f32[2,8,128]{2,1,0:T(8,128)S(1)} %get-tuple-element.44, (bf16[32,8,128]{2,1,0:T(8,128)(2,1)S(1)}, bf16[16,16,128]{2,1,0:T(8,128)(2,1)S(1)}, f32[2,8,128]{2,1,0:T(8,128)S(1)}, f32[2,2,128]{2,1,0:T(2,128)S(1)}, ...), branch_computations={%region_0.0_spmd, %region_1.0_spmd} | conditional | bytes 65544 | solution.py:301
  44.2 0.3 branch_1_fun.2
  44.5 9.2 %all_to_all.24.refs_0_ = bf16[16,8,128]{2,1,0:T(8,128)(2,1)S(1)} all-to-all(bf16[16,8,128]{2,1,0:T(8,128)(2,1)S(1)} %get-tuple-element.24), channel_id=1, replica_groups=mesh['sweep'=2,'xsec'=16] {'xsec'}, dimensions={0} | all-to-all | bytes 65536 | tf_op jit(solution)/shard_map/cond/branch_1_fun/all_to_all | solution.py:228
  53.7 0.2 branch_1_fun.3
  54.0 0.0 copy-start
  54.0 0.6 %copy-done = f32[2,8,128]{2,1,0:T(8,128)} copy-done((f32[2,8,128]{2,1,0:T(8,128)}, f32[2,8,128]{2,1,0:T(8,128)S(1)}, u32[]{:S(2)}) %copy-start) | copy-done | bytes 8216
Async XLA Ops:
  35.1 9.1 %all-to-all-start.4 = ((bf16[32,8,128]{2,1,0:T(8,128)(2,1)}), bf16[32,8,128]{2,1,0:T(8,128)(2,1)S(1)}, u32[]{:S(2)}, u32[]{:S(2)}) async-start(bf16[32,8,128]{2,1,0:T(8,128)(2,1)} %get-tuple-element.45), calls=%async_computation.4 | async-start | bytes 131072 | tf_op jit(solution)/shard_map/all_to_all | solution.py:228
  54.0 0.6 %copy-start = (f32[2,8,128]{2,1,0:T(8,128)}, f32[2,8,128]{2,1,0:T(8,128)S(1)}, u32[]{:S(2)}) copy-start(f32[2,8,128]{2,1,0:T(8,128)S(1)} %get-tuple-element.50) | copy-start | bytes 24580

commit v5 on v4

--- a/solution.py
+++ b/solution.py
@@ -165,13 +165,14 @@
     if row_at is None:
         whole, loads, coupling, schur, out, solved_out = refs
     else:
-        everyone, whole, loads, coupling, schur, out, solved_out = refs
+        everyone, whole, loads, coupling, schur, out, solved_out, row_out = refs
     peers = whole.shape[0]
     count = loads.shape[1]
     if row_at is not None:
         row = lax.axis_index(row_at)
         start = jnp.maximum(row - 1, 0) * peers
         keep = (row > 0).astype(F32)
+        row_out[0] = row
     blocks = []
     for peer in range(peers):
         piece = whole[peer].astype(F32)
@@ -218,7 +219,9 @@
         kernel,
         out_shape=out_shape,
         in_specs=[pl.BlockSpec(memory_space=space)] * len(operands),
-        out_specs=jax.tree.map(lambda _: pl.BlockSpec(memory_space=pltpu.VMEM), out_shape),
+        out_specs=jax.tree.map(
+            lambda out: pl.BlockSpec(memory_space=getattr(out, "memory_space", None) or pltpu.VMEM), out_shape
+        ),
         scratch_shapes=list(scratch),
         compiler_params=pltpu.CompilerParams(vmem_limit_bytes=16 * 1024 * 1024),
     )(*operands)
@@ -268,15 +271,20 @@
     whole = exchange(block, "xsec")
     gathered_shape = struct((peers, count, width), BF16)
     solved_shape = struct((count, width), F32)
-    whole_out = struct((layers, count, width), F32)
-
-    def solve_round(everyone, whole, loads, coupling, schur_inv, send):
-        behind = () if everyone is None else (everyone,)
-        block, solved = call(
-            functools.partial(round_kernel, row_at="sweep" if behind else None),
-            (gathered_shape, solved_shape),
-            behind + (whole, loads, coupling, schur_inv),
+    whole_out = pltpu.VMEM((layers, count, width), F32)
+
+    def first_layer(everyone, *operands):
+        if everyone is None:
+            return call(
+                functools.partial(round_kernel, row_at=None), (gathered_shape, solved_shape), operands
+            )
+        return call(
+            functools.partial(round_kernel, row_at="sweep"),
+            (gathered_shape, solved_shape, pltpu.SMEM((1,), jnp.int32)),
+            (everyone, *operands),
         )
+
+    def other_layers(block, solved, loads, coupling, schur_inv, send):
         done = [solved]
         for layer in range(1, layers - 1):
             block, solved = call(
@@ -292,17 +300,20 @@
             (exchange(block, "xsec"), *done, schur_inv),
         )
 
-    everyone = solved = None
+    everyone = None
     for round_at in range(chain - 1):
-        solved, block = solve_round(everyone, whole, loads, coupling, schur_inv, True)
+        block, solved = first_layer(everyone, whole, loads, coupling, schur_inv)[:2]
+        finished, block = other_layers(block, solved, loads, coupling, schur_inv, True)
         everyone = exchange(block, ("sweep", "xsec"))
     if chain == 1:
-        return solve_round(None, whole, loads, coupling, schur_inv, False)[0]
+        block, solved = first_layer(None, whole, loads, coupling, schur_inv)
+        return other_layers(block, solved, loads, coupling, schur_inv, False)[0]
+    block, solved, row = first_layer(everyone, whole, loads, coupling, schur_inv)
     return lax.cond(
-        lax.axis_index("sweep") == chain - 1,
-        lambda solved, *rest: solve_round(*rest, False)[0],
-        lambda solved, *rest: solved,
-        solved, everyone, whole, loads, coupling, schur_inv,
+        row[0] == chain - 1,
+        lambda finished, *rest: other_layers(*rest, False)[0],
+        lambda finished, *rest: finished,
+        finished, block, solved, loads, coupling, schur_inv,
     )
 
 

time: 54.9 us -> 53.4 us (0.973)
  blocking collectives: 40.5 us -> 48.8 us
  waiting for transfers between devices: 6.42 us -> 0 us
  starting transfers between devices: 2.67 us -> 0 us
  Pallas kernels: 4.31 us -> 3.68 us
    all_to_all x4 -> x5, blocking collectives: 40.5 us -> 48.8 us  [exchange(): return lax.all_to_all(blocks, axes, split_axis=0, concat_axis=0, tiled=True)]
    all_to_all x1 -> x0, waiting for transfers between devices: 6.42 us -> none  [exchange(): return lax.all_to_all(blocks, axes, split_axis=0, concat_axis=0, tiled=True)]
    all_to_all x1 -> x0, starting transfers between devices: 2.67 us -> none  [exchange(): return lax.all_to_all(blocks, axes, split_axis=0, concat_axis=0, tiled=True)]
    pallas_call x6, Pallas kernels: 4.31 us -> 3.68 us  [call(): pl.pallas_call(kernel, out_shape=out_shape, in_specs=[pl.BlockSpec(memory...]
  transfers between devices with their start and end apart: 1 -> 0, of which waited for: 1 -> 0; matrix products, arithmetic and copies ran while one was open for 0% -> 0% of each run, Pallas kernels for 0% -> 0%
where the time goes in v5:
time: 53.4 us; the launch traced here: 53.1 us
  blocking collectives  48.8 us (91%)
  Pallas kernels  3.68 us (7%)
  local copies, waits for them, and re-layouts  0.62 us (1%)
    all_to_all x5, blocking collectives, exchange(): return lax.all_to_all(blocks, axes, split_axis=0, concat_axis=0, tiled=True)  48.8 us
    pallas_call x6, Pallas kernels, call(): pl.pallas_call(kernel, out_shape=out_shape, in_specs=[pl.BlockSpec(memory...  3.68 us

profile of v5, /device:TPU:4, one launch (start us, length us, event | category | flops | bytes accessed | tf_op | source)
XLA Modules:
  0.0 53.1 jit_solution(11057034494330499422)
XLA Ops:
  0.0 2.0 %shard_map.66 = (bf16[16,8,192]{2,1,0:T(8,128)(2,1)S(1)}, s32[16,192]{1,0:T(8,128)S(1)}, f32[2,2,128]{2,1,0:T(2,128)S(1)}, bf16[2,2,2048,128]{3,2,1,0:T(8,128)(2,1)S(1)}) custom-call(bf16[2,24,40,128]{3,2,1,0:T(8,128)(2,1)} %bitcast.5, bf16[2,4,40,128]{3,2,1,0:T(8,128)(2,1)} %bitcast.6, s32[16,192]{1,0:T(8,128)} %bitcast.7, s32[16]{0:T(128)} %bitcast.8, ...), custom_call_target="tpu_custom_call" | custom-call | tf_op jit(solution)/shard_map/pallas_call | solution.py:218
  2.0 12.6 %all_to_all.25.received = bf16[16,8,192]{2,1,0:T(8,128)(2,1)S(1)} all-to-all(bf16[16,8,192]{2,1,0:T(8,128)(2,1)S(1)} %get-tuple-element.31), channel_id=1, replica_groups=mesh['sweep'=2,'xsec'=16] {'xsec'}, dimensions={0} | all-to-all | bytes 98304 | tf_op jit(solution)/shard_map/all_to_all | solution.py:231
  14.6 0.6 %shard_map.67 = (f32[2,8,128]{2,1,0:T(8,128)S(1)}, bf16[16,16,128]{2,1,0:T(8,128)(2,1)S(1)}) custom-call(bf16[16,8,192]{2,1,0:T(8,128)(2,1)S(1)} %all_to_all.25.received, s32[16,192]{1,0:T(8,128)S(1)} %get-tuple-element.32.index_rows, f32[2,2,128]{2,1,0:T(2,128)S(1)} %get-tuple-element.33.coupling.refs_2_.refs_3_), custom_call_target="tpu_custom_call" | custom-call | tf_op jit(solution)/shard_map/pallas_call | solution.py:218
  15.3 9.5 %all_to_all.26.refs_0_.refs_1_ = bf16[16,16,128]{2,1,0:T(8,128)(2,1)S(1)} all-to-all(bf16[16,16,128]{2,1,0:T(8,128)(2,1)S(1)} %get-tuple-element.34), channel_id=1, replica_groups=mesh['sweep'=2,'xsec'=16] {'xsec'}, dimensions={0} | all-to-all | bytes 131072 | tf_op jit(solution)/shard_map/all_to_all | solution.py:231
  24.8 0.3 shard_map.68
  25.0 9.2 %all_to_all.27.refs_0_ = bf16[16,8,128]{2,1,0:T(8,128)(2,1)S(1)} all-to-all(bf16[16,8,128]{2,1,0:T(8,128)(2,1)S(1)} %get-tuple-element.37), channel_id=1, replica_groups=mesh['sweep'=2,'xsec'=16] {'xsec'}, dimensions={0} | all-to-all | bytes 65536 | tf_op jit(solution)/shard_map/all_to_all | solution.py:231
  34.2 0.2 shard_map.69
  34.5 8.3 %all_to_all.28.refs_0_ = bf16[32,8,128]{2,1,0:T(8,128)(2,1)S(1)} all-to-all(bf16[32,8,128]{2,1,0:T(8,128)(2,1)S(1)} %get-tuple-element.39), channel_id=1, replica_groups=mesh['sweep'=2,'xsec'=16] {'sweep','xsec'}, dimensions={0} | all-to-all | bytes 131072 | tf_op jit(solution)/shard_map/all_to_all | solution.py:231
  42.8 0.3 shard_map.70
  43.0 9.5 %conditional.1 = (f32[2,8,128]{2,1,0:T(8,128)S(1)}) conditional(s32[]{:T(128)} %bitcast.4, f32[2,8,128]{2,1,0:T(8,128)S(1)} %get-tuple-element.41, (bf16[16,8,128]{2,1,0:T(8,128)(2,1)S(1)}, f32[8,128]{1,0:T(8,128)S(1)}, bf16[2,2,2048,128]{3,2,1,0:T(8,128)(2,1)S(1)}) %tuple.11), branch_computations={%region_0.0_spmd, %region_1.0_spmd} | conditional | bytes 65544 | solution.py:312
  43.1 9.2 %all_to_all.24.refs_0_ = bf16[16,8,128]{2,1,0:T(8,128)(2,1)S(1)} all-to-all(bf16[16,8,128]{2,1,0:T(8,128)(2,1)S(1)} %get-tuple-element.15), channel_id=1, replica_groups=mesh['sweep'=2,'xsec'=16] {'xsec'}, dimensions={0} | all-to-all | bytes 65536 | tf_op jit(solution)/shard_map/cond/branch_1_fun/all_to_all | solution.py:231
  52.3 0.2 branch_1_fun.1
  52.5 0.6 %copy.11 = f32[2,8,128]{2,1,0:T(8,128)} copy(f32[2,8,128]{2,1,0:T(8,128)S(1)} %get-tuple-element.44) | data formatting | bytes 16384

commit v6 on v5

v6 whole, which is shorter than its diff:
```python
import functools

import jax
import jax.numpy as jnp
from jax import lax
from jax.experimental import pallas as pl
from jax.experimental.pallas import tpu as pltpu
from jax.sharding import PartitionSpec as P

CAP = 8
LANES = 128
CHUNKS = 2
F32 = jnp.float32
BF16 = jnp.bfloat16


def iota(shape, axis):
    return lax.broadcasted_iota(jnp.int32, shape, axis)


def sum_sublanes(tiles):
    sub = iota((8, LANES), 0)
    low = sub < 4
    halves = [
        jnp.where(low, tiles[r], tiles[r + 4]) + pltpu.roll(jnp.where(low, tiles[r + 4], tiles[r]), 4, 0)
        for r in range(4)
    ]

    def fold(first, second, step):
        even = (sub & step) == 0
        return jnp.where(even, first, second) + jnp.where(
            even, pltpu.roll(first, 8 - step, 0), pltpu.roll(second, step, 0)
        )

    pairs = [fold(halves[r], halves[r + 2], 2) for r in range(2)]
    return fold(pairs[0], pairs[1], 1)


def skew_block(tile, at, group):
    shift = at * group % LANES
    return pltpu.roll(tile, shift, 1) if shift else tile


def unskew_blocks(tiles, group):
    count = len(tiles)
    lane = iota((8, LANES), 1) // group
    tiles = list(tiles)
    bit = 1
    while bit < count:
        take = (lane & bit) != 0
        tiles = [jnp.where(take, tiles[(at + bit) % count], tiles[at]) for at in range(count)]
        bit *= 2
    return [skew_block(tiles[-at % count], LANES // group - at, group) for at in range(count)]


def pack_coupling(layer, rows):
    high = layer.astype(BF16).astype(F32)
    both = jnp.concatenate([high, layer - high], 0)
    lanes = both.shape[0] * both.shape[1] // rows
    return jnp.concatenate([both[:, at : at + lanes] for at in range(0, both.shape[1], lanes)], 0)


def unpack_coupling(packed):
    both = jnp.concatenate([packed[at : at + 4] for at in range(0, packed.shape[0], 4)], 1)
    return both[:2] + both[2:]


def contract_kernel(
    cond_hbm, source_hbm, index_hbm, counts_hbm, coupling_hbm, schur_hbm,
    out, place_out, layer_out, coupling_out, schur_out,
    cond, source, index_rows, counts, source32, sems,
):
    _, n_faces, n_inner, elems = cond.shape
    sources = source.shape[1]
    owners = LANES // CAP
    faces_each = n_faces // CHUNKS
    width = coupling_out.shape[2]
    groups = []
    while len(groups) < n_faces:
        size = owners
        while size > n_faces - len(groups):
            size //= 2
        groups += [(len(groups), size)] * size
    early = [
        pltpu.make_async_copy(source_hbm, source, sems.at[0]),
        pltpu.make_async_copy(index_hbm, index_rows, sems.at[1]),
        pltpu.make_async_copy(counts_hbm, counts, sems.at[2]),
    ]
    chunks = []
    for chunk in range(CHUNKS):
        some = pl.ds(chunk * faces_each, faces_each)
        chunks.append(pltpu.make_async_copy(cond_hbm.at[:, some], cond.at[:, some], sems.at[3 + chunk]))
    late = [
        pltpu.make_async_copy(coupling_hbm, coupling_out, sems.at[3 + CHUNKS]),
        pltpu.make_async_copy(schur_hbm, schur_out, sems.at[4 + CHUNKS]),
    ]
    for copy in early + chunks + late:
        copy.start()
    for copy in early:
        copy.wait()
    position = iota((1, index_rows.shape[1]), 1) % CAP
    for sender in range(index_rows.shape[0]):
        row = index_rows[sender : sender + 1, :]
        live = position < counts[sender]
        place_out[sender : sender + 1, :] = jnp.where(live, row % width, -1)
        layer_out[sender : sender + 1, :] = row // width
    for block in range(elems // LANES):
        lanes = pl.ds(block * LANES, LANES)
        source32[:2] = source[:, :, :, lanes].astype(F32)
        source32[2] = source32[0] + source32[1]
        parts = [[] for _ in range(owners)]
        skewed = []
        for face in range(n_faces):
            if block == 0 and face % faces_each == 0:
                chunks[face // faces_each].wait()
            left_re = cond[0, face, :, lanes].astype(F32)
            left_im = cond[1, face, :, lanes].astype(F32)
            left_sum = left_re + left_im
            left_gap = left_im - left_re
            tiles = [None] * (2 * sources)
            for j in range(sources):
                both = jnp.sum((left_re * source32[2, j]).reshape(n_inner // 8, 8, LANES), 0)
                minus = jnp.sum((left_sum * source32[1, j]).reshape(n_inner // 8, 8, LANES), 0)
                plus = jnp.sum((left_gap * source32[0, j]).reshape(n_inner // 8, 8, LANES), 0)
                tiles[j] = both - minus
                tiles[sources + j] = both + plus
            first, size = groups[face]
            skewed.append(skew_block(sum_sublanes(tiles), face - first, CAP))
            if len(skewed) < size:
                continue
            moved = unskew_blocks(skewed, CAP)
            skewed = []
            for owner in range(owners):
                piece = moved[owner % size]
                if owner >= size:
                    piece = skew_block(piece, owners - owner // size * size, CAP)
                parts[owner].append(piece[:, : size * CAP])
        if block == 0:
            late[0].wait()
            spare = pack_coupling(coupling_out[0], 2 * sources)
        for owner in range(owners):
            out[block * owners + owner] = jnp.concatenate(parts[owner] + [spare], 1).astype(BF16)
    late[1].wait()


def assemble_kernel(received, place_rows, layer_rows, coupling, loads, out):
    peers, rows, _ = received.shape
    face_rows = place_rows.shape[1]
    layers, _, width = loads.shape
    place = iota((width, face_rows), 0)
    total = jnp.zeros((layers * rows, width), F32)
    for sender in range(peers):
        onehot = jnp.where(place == place_rows[sender : sender + 1, :], 1.0, 0.0).astype(BF16)
        values = received[sender].astype(F32)[:, :face_rows]
        layer_row = layer_rows[sender : sender + 1, :]
        split = [jnp.where(layer_row == layer, values, 0.0) for layer in range(layers)]
        total += lax.dot_general(
            jnp.concatenate(split, 0).astype(BF16), onehot, (((1,), (1,)), ((), ())), preferred_element_type=F32
        )
    for layer in range(layers):
        loads[layer] = total[layer * rows : (layer + 1) * rows]
    block = couple(total[:rows], coupling[0], jnp.zeros((rows, width), F32)).astype(BF16)
    for peer in range(out.shape[0]):
        out[peer] = block


def couple(loads, coupling, carried):
    half = loads.shape[0] // 2
    couple_re, couple_im = coupling[0:1], coupling[1:2]
    real, imag = carried[:half], carried[half:]
    return jnp.concatenate(
        [
            loads[:half] - (couple_re * real - couple_im * imag),
            loads[half:] - (couple_re * imag + couple_im * real),
        ],
        0,
    )


def apply_schur(rhs, schur, layer):
    half = rhs.shape[0] // 2
    first = jnp.dot(rhs, schur[layer, 0], preferred_element_type=F32)
    second = jnp.dot(rhs, schur[layer, 1], preferred_element_type=F32)
    return jnp.concatenate([first[:half] - second[half:], second[:half] + first[half:]], 0)


def cross_kernel(everyone, whole, received, loads, coupling, schur, out, solved_out, row_out, *, row_axis):
    peers = whole.shape[0]
    _, count, width = loads.shape
    spare = received.shape[2] - 4 * width // count
    row = lax.axis_index(row_axis)
    row_out[0] = row
    start = jnp.maximum(row - 1, 0) * peers
    keep = (row > 0).astype(F32)
    blocks = []
    for peer in range(peers):
        pair = unpack_coupling(received[peer].astype(F32)[:, spare:])
        before = everyone[start + peer].astype(F32) * keep
        blocks.append(couple(whole[peer].astype(F32), pair, before).astype(BF16))
    solved = apply_schur(jnp.concatenate(blocks, 1), schur, 0)
    solved_out[...] = solved
    block = couple(loads[1], coupling[1], solved).astype(BF16)
    for peer in range(out.shape[0]):
        out[peer] = block


def layer_kernel(gathered, loads, coupling, schur, out, solved_out, *, layer):
    rhs = jnp.concatenate([gathered[peer] for peer in range(gathered.shape[0])], 1)
    solved = apply_schur(rhs, schur, layer)
    solved_out[...] = solved
    block = couple(loads[layer + 1], coupling[layer + 1], solved).astype(BF16)
    for peer in range(out.shape[0]):
        out[peer] = block


def last_kernel(*refs, layer, send):
    gathered, *earlier, schur = refs[: layer + 2]
    outs = refs[layer + 2 :]
    rhs = jnp.concatenate([gathered[peer] for peer in range(gathered.shape[0])], 1)
    solved = apply_schur(rhs, schur, layer)
    for at in range(layer):
        outs[0][at] = earlier[at][...]
    outs[0][layer] = solved
    if send:
        block = solved.astype(BF16)
        for peer in range(outs[1].shape[0]):
            outs[1][peer] = block


def call(kernel, out_shape, operands, scratch=(), space=pltpu.VMEM):
    if space == pltpu.HBM:
        operands = [pltpu.with_memory_space_constraint(operand, space) for operand in operands]
    return pl.pallas_call(
        kernel,
        out_shape=out_shape,
        in_specs=[pl.BlockSpec(memory_space=space)] * len(operands),
        out_specs=jax.tree.map(
            lambda out: pl.BlockSpec(memory_space=getattr(out, "memory_space", None) or pltpu.VMEM), out_shape
        ),
        scratch_shapes=list(scratch),
        compiler_params=pltpu.CompilerParams(vmem_limit_bytes=16 * 1024 * 1024),
    )(*operands)


def exchange(blocks, axes):
    return lax.all_to_all(blocks, axes, split_axis=0, concat_axis=0, tiled=True)


def shards(cond_block, interior_src, face_index, owner_count, coupling, schur_inv):
    layers = schur_inv.shape[0]
    width = schur_inv.shape[3]
    sources = interior_src.shape[3]
    n_faces, n_inner, elems = cond_block.shape[3:]
    peers = lax.axis_size("xsec")
    chain = lax.axis_size("sweep")
    count = 2 * sources
    struct = jax.ShapeDtypeStruct
    gathered_shape = struct((peers, count, width), BF16)

    index_rows = face_index[0, 0]
    outgoing, place_rows, layer_rows, coupling, schur_inv = call(
        contract_kernel,
        (
            struct((peers, count, n_faces * CAP + 4 * width // count), BF16),
            struct(index_rows.shape, index_rows.dtype),
            struct(index_rows.shape, index_rows.dtype),
            struct(coupling.shape, coupling.dtype),
            struct(schur_inv.shape, schur_inv.dtype),
        ),
        (cond_block[0, 0], interior_src[0, 0], index_rows, owner_count[0, 0], coupling, schur_inv),
        scratch=(
            pltpu.VMEM(cond_block.shape[2:], BF16),
            pltpu.VMEM(interior_src.shape[2:], BF16),
            pltpu.VMEM(index_rows.shape, index_rows.dtype),
            pltpu.SMEM(owner_count.shape[2:], owner_count.dtype),
            pltpu.VMEM((3, sources, n_inner, LANES), F32),
            pltpu.SemaphoreType.DMA((5 + CHUNKS,)),
        ),
        space=pltpu.HBM,
    )
    received = exchange(outgoing, "xsec")
    loads, block = call(
        assemble_kernel,
        (struct((layers, count, width), F32), gathered_shape),
        (received, place_rows, layer_rows, coupling),
    )
    whole = exchange(block, "xsec")
    solved_shape = struct((count, width), F32)
    whole_out = pltpu.VMEM((layers, count, width), F32)

    def next_layers(gathered, loads, coupling, schur_inv, done, send):
        for layer in range(len(done), layers - 1):
            block, solved = call(
                functools.partial(layer_kernel, layer=layer),
                (gathered_shape, solved_shape),
                (gathered, loads, coupling, schur_inv),
            )
            done = done + [solved]
            gathered = exchange(block, "xsec")
        sent = (struct((chain * peers, count, width), BF16),) if send else ()
        return call(
            functools.partial(last_kernel, layer=layers - 1, send=send),
            (whole_out,) + sent,
            (gathered, *done, schur_inv),
        )

    def later_round(everyone):
        return call(
            functools.partial(cross_kernel, row_axis="sweep"),
            (gathered_shape, solved_shape, pltpu.SMEM((1,), jnp.int32)),
            (everyone, whole, received, loads, coupling, schur_inv),
        )

    if chain == 1:
        return next_layers(whole, loads, coupling, schur_inv, [], False)[0]
    finished, block = next_layers(whole, loads, coupling, schur_inv, [], True)
    for _ in range(chain - 2):
        block, solved, _ = later_round(exchange(block, ("sweep", "xsec")))
        finished, block = next_layers(
            exchange(block, "xsec"), loads, coupling, schur_inv, [solved], True
        )
    block, solved, row = later_round(exchange(block, ("sweep", "xsec")))

    def last_round(finished, block, solved, loads, coupling, schur_inv):
        return next_layers(exchange(block, "xsec"), loads, coupling, schur_inv, [solved], False)[0]

    return lax.cond(
        row[0] == chain - 1,
        last_round,
        lambda finished, *rest: finished,
        finished, block, solved, loads, coupling, schur_inv,
    )


def solution(mesh):
    placed = (
        P("sweep", "xsec", None, None, None, None),
        P("sweep", "xsec", None, None, None, None),
        P("sweep", "xsec", None, None),
        P("sweep", "xsec", None),
        P("sweep", None, "xsec"),
        P("sweep", None, None, "xsec"),
    )
    return jax.shard_map(
        shards, mesh=mesh, in_specs=placed, out_specs=P("sweep", None, "xsec"), check_vma=False
    )
```

time: 53.4 us -> 52.9 us (level)
  no operation moved by 1% of the time
where the time goes in v6:
time: 52.9 us; the launch traced here: 52.6 us
  blocking collectives  48.5 us (92%)
  Pallas kernels  3.44 us (7%)
  local copies, waits for them, and re-layouts  0.62 us (1%)
    all_to_all x5, blocking collectives, exchange(): return lax.all_to_all(blocks, axes, split_axis=0, concat_axis=0, tiled=True)  48.5 us
    pallas_call x6, Pallas kernels, call(): pl.pallas_call(kernel, out_shape=out_shape, in_specs=[pl.BlockSpec(memory...  3.44 us

profile of v6, /device:TPU:4, one launch (start us, length us, event | category | flops | bytes accessed | tf_op | source)
XLA Modules:
  0.0 52.6 jit_solution(3761713880981011845)
XLA Ops:
  0.0 2.0 %shard_map.66 = (bf16[16,8,256]{2,1,0:T(8,128)(2,1)S(1)}, s32[16,192]{1,0:T(8,128)S(1)}, s32[16,192]{1,0:T(8,128)S(1)}, f32[2,2,128]{2,1,0:T(2,128)S(1)}, bf16[2,2,2048,128]{3,2,1,0:T(8,128)(2,1)S(1)}) custom-call(bf16[2,24,40,128]{3,2,1,0:T(8,128)(2,1)} %bitcast.5, bf16[2,4,40,128]{3,2,1,0:T(8,128)(2,1)} %bitcast.6, s32[16,192]{1,0:T(8,128)} %bitcast.7, ...), custom_call_target="tpu_custom_call" | custom-call | tf_op jit(solution)/shard_map/pallas_call | solution.py:233
  2.0 12.6 %all_to_all.25.received = bf16[16,8,256]{2,1,0:T(8,128)(2,1)S(1)} all-to-all(bf16[16,8,256]{2,1,0:T(8,128)(2,1)S(1)} %get-tuple-element.32), channel_id=1, replica_groups=mesh['sweep'=2,'xsec'=16] {'xsec'}, dimensions={0} | all-to-all | bytes 131072 | tf_op jit(solution)/shard_map/all_to_all | solution.py:246
  14.6 0.4 shard_map.67
  15.0 9.2 %all_to_all.26.gathered.whole = bf16[16,8,128]{2,1,0:T(8,128)(2,1)S(1)} all-to-all(bf16[16,8,128]{2,1,0:T(8,128)(2,1)S(1)} %get-tuple-element.36), channel_id=1, replica_groups=mesh['sweep'=2,'xsec'=16] {'xsec'}, dimensions={0} | all-to-all | bytes 65536 | tf_op jit(solution)/shard_map/all_to_all | solution.py:246
  24.2 0.3 shard_map.68
  24.5 9.2 %all_to_all.27.refs_0_ = bf16[16,8,128]{2,1,0:T(8,128)(2,1)S(1)} all-to-all(bf16[16,8,128]{2,1,0:T(8,128)(2,1)S(1)} %get-tuple-element.39), channel_id=1, replica_groups=mesh['sweep'=2,'xsec'=16] {'xsec'}, dimensions={0} | all-to-all | bytes 65536 | tf_op jit(solution)/shard_map/all_to_all | solution.py:246
  33.7 0.2 shard_map.69
  33.9 8.3 %all_to_all.28.everyone = bf16[32,8,128]{2,1,0:T(8,128)(2,1)S(1)} all-to-all(bf16[32,8,128]{2,1,0:T(8,128)(2,1)S(1)} %get-tuple-element.41), channel_id=1, replica_groups=mesh['sweep'=2,'xsec'=16] {'sweep','xsec'}, dimensions={0} | all-to-all | bytes 131072 | tf_op jit(solution)/shard_map/all_to_all | solution.py:246
  42.2 0.3 shard_map.70
  42.5 9.5 %conditional.1 = (f32[2,8,128]{2,1,0:T(8,128)S(1)}) conditional(s32[]{:T(128)} %bitcast.4, f32[2,8,128]{2,1,0:T(8,128)S(1)} %get-tuple-element.43, (bf16[16,8,128]{2,1,0:T(8,128)(2,1)S(1)}, f32[8,128]{1,0:T(8,128)S(1)}, bf16[2,2,2048,128]{3,2,1,0:T(8,128)(2,1)S(1)}) %tuple.11), branch_computations={%region_0.0_spmd, %region_1.0_spmd} | conditional | bytes 65544 | solution.py:327
  42.5 9.2 %all_to_all.24.refs_0_ = bf16[16,8,128]{2,1,0:T(8,128)(2,1)S(1)} all-to-all(bf16[16,8,128]{2,1,0:T(8,128)(2,1)S(1)} %get-tuple-element.15), channel_id=1, replica_groups=mesh['sweep'=2,'xsec'=16] {'xsec'}, dimensions={0} | all-to-all | bytes 65536 | tf_op jit(solution)/shard_map/cond/branch_1_fun/all_to_all | solution.py:246
  51.7 0.2 branch_1_fun.1
  52.0 0.6 %copy.11 = f32[2,8,128]{2,1,0:T(8,128)} copy(f32[2,8,128]{2,1,0:T(8,128)S(1)} %get-tuple-element.46) | data formatting | bytes 16384

commit v7 on v6

--- a/solution.py
+++ b/solution.py
@@ -12,6 +12,14 @@
 CHUNKS = 2
 F32 = jnp.float32
 BF16 = jnp.bfloat16
+
+
+def first_of(count):
+    return (count // 2 + 1) % count
+
+
+def place_of(device, count):
+    return (device - first_of(count)) % count
 
 
 def iota(shape, axis):
@@ -139,7 +147,7 @@
             late[0].wait()
             spare = pack_coupling(coupling_out[0], 2 * sources)
         for owner in range(owners):
-            out[block * owners + owner] = jnp.concatenate(parts[owner] + [spare], 1).astype(BF16)
+            out[place_of(block * owners + owner, out.shape[0])] = jnp.concatenate(parts[owner] + [spare], 1).astype(BF16)
     late[1].wait()
 
 
@@ -151,7 +159,7 @@
     total = jnp.zeros((layers * rows, width), F32)
     for sender in range(peers):
         onehot = jnp.where(place == place_rows[sender : sender + 1, :], 1.0, 0.0).astype(BF16)
-        values = received[sender].astype(F32)[:, :face_rows]
+        values = received[place_of(sender, peers)].astype(F32)[:, :face_rows]
         layer_row = layer_rows[sender : sender + 1, :]
         split = [jnp.where(layer_row == layer, values, 0.0) for layer in range(layers)]
         total += lax.dot_general(
@@ -194,9 +202,10 @@
     keep = (row > 0).astype(F32)
     blocks = []
     for peer in range(peers):
-        pair = unpack_coupling(received[peer].astype(F32)[:, spare:])
+        place = place_of(peer, peers)
+        pair = unpack_coupling(received[place].astype(F32)[:, spare:])
         before = everyone[start + peer].astype(F32) * keep
-        blocks.append(couple(whole[peer].astype(F32), pair, before).astype(BF16))
+        blocks.append(couple(whole[place].astype(F32), pair, before).astype(BF16))
     solved = apply_schur(jnp.concatenate(blocks, 1), schur, 0)
     solved_out[...] = solved
     block = couple(loads[1], coupling[1], solved).astype(BF16)
@@ -204,8 +213,13 @@
         out[peer] = block
 
 
+def side_by_side(gathered):
+    count = gathered.shape[0]
+    return jnp.concatenate([gathered[place_of(peer, count)] for peer in range(count)], 1)
+
+
 def layer_kernel(gathered, loads, coupling, schur, out, solved_out, *, layer):
-    rhs = jnp.concatenate([gathered[peer] for peer in range(gathered.shape[0])], 1)
+    rhs = side_by_side(gathered)
     solved = apply_schur(rhs, schur, layer)
     solved_out[...] = solved
     block = couple(loads[layer + 1], coupling[layer + 1], solved).astype(BF16)
@@ -216,7 +230,7 @@
 def last_kernel(*refs, layer, send):
     gathered, *earlier, schur = refs[: layer + 2]
     outs = refs[layer + 2 :]
-    rhs = jnp.concatenate([gathered[peer] for peer in range(gathered.shape[0])], 1)
+    rhs = side_by_side(gathered)
     solved = apply_schur(rhs, schur, layer)
     for at in range(layer):
         outs[0][at] = earlier[at][...]
@@ -242,8 +256,16 @@
     )(*operands)
 
 
-def exchange(blocks, axes):
-    return lax.all_to_all(blocks, axes, split_axis=0, concat_axis=0, tiled=True)
+def exchange_row(blocks):
+    count = blocks.shape[0]
+    order = [(first_of(count) + place) % count for place in range(count)]
+    return lax.all_to_all(
+        blocks, "xsec", split_axis=0, concat_axis=0, tiled=True, axis_index_groups=[order]
+    )
+
+
+def exchange_all(blocks):
+    return lax.all_to_all(blocks, ("sweep", "xsec"), split_axis=0, concat_axis=0, tiled=True)
 
 
 def shards(cond_block, interior_src, face_index, owner_count, coupling, schur_inv):
@@ -278,13 +300,13 @@
         ),
         space=pltpu.HBM,
     )
-    received = exchange(outgoing, "xsec")
+    received = exchange_row(outgoing)
     loads, block = call(
         assemble_kernel,
         (struct((layers, count, width), F32), gathered_shape),
         (received, place_rows, layer_rows, coupling),
     )
-    whole = exchange(block, "xsec")
+    whole = exchange_row(block)
     solved_shape = struct((count, width), F32)
     whole_out = pltpu.VMEM((layers, count, width), F32)
 
@@ -296,7 +318,7 @@
                 (gathered, loads, coupling, schur_inv),
             )
             done = done + [solved]
-            gathered = exchange(block, "xsec")
+            gathered = exchange_row(block)
         sent = (struct((chain * peers, count, width), BF16),) if send else ()
         return call(
             functools.partial(last_kernel, layer=layers - 1, send=send),
@@ -315,14 +337,14 @@
         return next_layers(whole, loads, coupling, schur_inv, [], False)[0]
     finished, block = next_layers(whole, loads, coupling, schur_inv, [], True)
     for _ in range(chain - 2):
-        block, solved, _ = later_round(exchange(block, ("sweep", "xsec")))
+        block, solved, _ = later_round(exchange_all(block))
         finished, block = next_layers(
-            exchange(block, "xsec"), loads, coupling, schur_inv, [solved], True
-        )
-    block, solved, row = later_round(exchange(block, ("sweep", "xsec")))
+            exchange_row(block), loads, coupling, schur_inv, [solved], True
+        )
+    block, solved, row = later_round(exchange_all(block))
 
     def last_round(finished, block, solved, loads, coupling, schur_inv):
-        return next_layers(exchange(block, "xsec"), loads, coupling, schur_inv, [solved], False)[0]
+        return next_layers(exchange_row(block), loads, coupling, schur_inv, [solved], False)[0]
 
     return lax.cond(
         row[0] == chain - 1,

time: 52.9 us -> 49.1 us (0.928)
  blocking collectives: 48.5 us -> 44.7 us
    all_to_all x5, blocking collectives: 48.5 us -> 44.7 us  [the longest x4 34.8 us: exchange_row(): lax.all_to_all(blocks, 'xsec', split_axis=0, concat_axis=0, tiled=True, a...]
where the time goes in v7:
time: 49.1 us; the launch traced here: 48.8 us
  blocking collectives  44.7 us (91%)
  Pallas kernels  3.44 us (7%)
  local copies, waits for them, and re-layouts  0.62 us (1%)
    all_to_all x4, blocking collectives, exchange_row(): lax.all_to_all(blocks, 'xsec', split_axis=0, concat_axis=0, tiled=True, a...  34.8 us
    all_to_all x1, blocking collectives, exchange_all(): lax.all_to_all(blocks, ('sweep', 'xsec'), split_axis=0, concat_axis=0, ti...  9.92 us
    pallas_call x6, Pallas kernels, call(): pl.pallas_call(kernel, out_shape=out_shape, in_specs=[pl.BlockSpec(memory...  3.44 us

profile of v7, /device:TPU:4, one launch (start us, length us, event | category | flops | bytes accessed | tf_op | source)
XLA Modules:
  0.0 48.8 jit_solution(1732376741046534604)
XLA Ops:
  0.0 2.0 %shard_map.66 = (bf16[16,8,256]{2,1,0:T(8,128)(2,1)S(1)}, s32[16,192]{1,0:T(8,128)S(1)}, s32[16,192]{1,0:T(8,128)S(1)}, f32[2,2,128]{2,1,0:T(2,128)S(1)}, bf16[2,2,2048,128]{3,2,1,0:T(8,128)(2,1)S(1)}) custom-call(bf16[2,24,40,128]{3,2,1,0:T(8,128)(2,1)} %bitcast.5, bf16[2,4,40,128]{3,2,1,0:T(8,128)(2,1)} %bitcast.6, s32[16,192]{1,0:T(8,128)} %bitcast.7, ...), custom_call_target="tpu_custom_call" | custom-call | tf_op jit(solution)/shard_map/pallas_call | solution.py:247
  2.0 10.5 %all_to_all.25.received = bf16[16,8,256]{2,1,0:T(8,128)(2,1)S(1)} all-to-all(bf16[16,8,256]{2,1,0:T(8,128)(2,1)S(1)} %get-tuple-element.32), channel_id=1, replica_groups={{9,10,11,12,13,14,15,0,1,2,3,4,5,6,7,8},{25,26,27,28,29,30,31,16,17,18,..., dimensions={0} | all-to-all | bytes 131072 | tf_op jit(solution)/shard_map/all_to_all | solution.py:262
  12.5 0.4 shard_map.67
  12.9 8.1 %all_to_all.26.gathered.whole = bf16[16,8,128]{2,1,0:T(8,128)(2,1)S(1)} all-to-all(bf16[16,8,128]{2,1,0:T(8,128)(2,1)S(1)} %get-tuple-element.36), channel_id=1, replica_groups={{9,10,11,12,13,14,15,0,1,2,3,4,5,6,7,8},{25,26,27,28,29,30,31,16,17,18,..., dimensions={0} | all-to-all | bytes 65536 | tf_op jit(solution)/shard_map/all_to_all | solution.py:262
  21.0 0.3 shard_map.68
  21.3 8.1 %all_to_all.27.refs_0_ = bf16[16,8,128]{2,1,0:T(8,128)(2,1)S(1)} all-to-all(bf16[16,8,128]{2,1,0:T(8,128)(2,1)S(1)} %get-tuple-element.39), channel_id=1, replica_groups={{9,10,11,12,13,14,15,0,1,2,3,4,5,6,7,8},{25,26,27,28,29,30,31,16,17,18,..., dimensions={0} | all-to-all | bytes 65536 | tf_op jit(solution)/shard_map/all_to_all | solution.py:262
  29.4 0.2 shard_map.69
  29.6 9.9 %all_to_all.28.everyone = bf16[32,8,128]{2,1,0:T(8,128)(2,1)S(1)} all-to-all(bf16[32,8,128]{2,1,0:T(8,128)(2,1)S(1)} %get-tuple-element.41), channel_id=1, replica_groups=mesh['sweep'=2,'xsec'=16] {'sweep','xsec'}, dimensions={0} | all-to-all | bytes 131072 | tf_op jit(solution)/shard_map/all_to_all | solution.py:268
  39.5 0.3 shard_map.70
  39.9 8.4 %conditional.1 = (f32[2,8,128]{2,1,0:T(8,128)S(1)}) conditional(s32[]{:T(128)} %bitcast.4, f32[2,8,128]{2,1,0:T(8,128)S(1)} %get-tuple-element.43, (bf16[16,8,128]{2,1,0:T(8,128)(2,1)S(1)}, f32[8,128]{1,0:T(8,128)S(1)}, bf16[2,2,2048,128]{3,2,1,0:T(8,128)(2,1)S(1)}) %tuple.11), branch_computations={%region_0.0_spmd, %region_1.0_spmd} | conditional | bytes 65544 | solution.py:349
  39.9 8.1 %all_to_all.24.refs_0_ = bf16[16,8,128]{2,1,0:T(8,128)(2,1)S(1)} all-to-all(bf16[16,8,128]{2,1,0:T(8,128)(2,1)S(1)} %get-tuple-element.15), channel_id=1, replica_groups={{9,10,11,12,13,14,15,0,1,2,3,4,5,6,7,8},{25,26,27,28,29,30,31,16,17,18,..., dimensions={0} | all-to-all | bytes 65536 | tf_op jit(solution)/shard_map/cond/branch_1_fun/all_to_all | solution.py:262
  48.0 0.2 branch_1_fun.1
  48.2 0.6 %copy.11 = f32[2,8,128]{2,1,0:T(8,128)} copy(f32[2,8,128]{2,1,0:T(8,128)S(1)} %get-tuple-element.46) | data formatting | bytes 16384

commit v8 on v7

--- a/solution.py
+++ b/solution.py
@@ -51,11 +51,11 @@
 
 def unskew_blocks(tiles, group):
     count = len(tiles)
-    lane = iota((8, LANES), 1) // group
+    lane = iota((8, LANES), 1)
     tiles = list(tiles)
     bit = 1
     while bit < count:
-        take = (lane & bit) != 0
+        take = (lane & (bit * group)) != 0
         tiles = [jnp.where(take, tiles[(at + bit) % count], tiles[at]) for at in range(count)]
         bit *= 2
     return [skew_block(tiles[-at % count], LANES // group - at, group) for at in range(count)]
@@ -82,7 +82,7 @@
     sources = source.shape[1]
     owners = LANES // CAP
     faces_each = n_faces // CHUNKS
-    width = coupling_out.shape[2]
+    layers, _, width = coupling_out.shape
     groups = []
     while len(groups) < n_faces:
         size = owners
@@ -109,9 +109,9 @@
     position = iota((1, index_rows.shape[1]), 1) % CAP
     for sender in range(index_rows.shape[0]):
         row = index_rows[sender : sender + 1, :]
-        live = position < counts[sender]
-        place_out[sender : sender + 1, :] = jnp.where(live, row % width, -1)
-        layer_out[sender : sender + 1, :] = row // width
+        layer = sum((row >= at * width).astype(jnp.int32) for at in range(1, layers))
+        place_out[sender : sender + 1, :] = jnp.where(position < counts[sender], row - layer * width, -1)
+        layer_out[sender : sender + 1, :] = layer
     for block in range(elems // LANES):
         lanes = pl.ds(block * LANES, LANES)
         source32[:2] = source[:, :, :, lanes].astype(F32)
@@ -218,7 +218,9 @@
     return jnp.concatenate([gathered[place_of(peer, count)] for peer in range(count)], 1)
 
 
-def layer_kernel(gathered, loads, coupling, schur, out, solved_out, *, layer):
+def layer_kernel(gathered, loads, coupling, schur, out, solved_out, *row_out, layer):
+    if row_out:
+        row_out[0][0] = lax.axis_index("sweep")
     rhs = side_by_side(gathered)
     solved = apply_schur(rhs, schur, layer)
     solved_out[...] = solved
@@ -310,48 +312,46 @@
     solved_shape = struct((count, width), F32)
     whole_out = pltpu.VMEM((layers, count, width), F32)
 
-    def next_layers(gathered, loads, coupling, schur_inv, done, send):
-        for layer in range(len(done), layers - 1):
+    row_shape = pltpu.SMEM((1,), jnp.int32)
+
+    def other_layers(block, solved, loads, coupling, schur_inv, send):
+        done = [solved]
+        for layer in range(1, layers - 1):
             block, solved = call(
                 functools.partial(layer_kernel, layer=layer),
                 (gathered_shape, solved_shape),
-                (gathered, loads, coupling, schur_inv),
+                (exchange_row(block), loads, coupling, schur_inv),
             )
-            done = done + [solved]
-            gathered = exchange_row(block)
+            done.append(solved)
         sent = (struct((chain * peers, count, width), BF16),) if send else ()
         return call(
             functools.partial(last_kernel, layer=layers - 1, send=send),
             (whole_out,) + sent,
-            (gathered, *done, schur_inv),
+            (exchange_row(block), *done, schur_inv),
         )
 
-    def later_round(everyone):
-        return call(
-            functools.partial(cross_kernel, row_axis="sweep"),
-            (gathered_shape, solved_shape, pltpu.SMEM((1,), jnp.int32)),
-            (everyone, whole, received, loads, coupling, schur_inv),
+    block, solved, row = call(
+        functools.partial(layer_kernel, layer=0),
+        (gathered_shape, solved_shape, row_shape),
+        (whole, loads, coupling, schur_inv),
+    )
+    finished = loads
+    for round_at in range(chain):
+        send = round_at < chain - 1
+        nothing = struct((chain * peers, count, width), BF16)
+        finished, *sent = lax.cond(
+            row[0] == round_at,
+            lambda finished, *rest: tuple(other_layers(*rest, send)),
+            lambda finished, *rest: (finished,) + ((jnp.zeros(nothing.shape, BF16),) if send else ()),
+            finished, block, solved, loads, coupling, schur_inv,
         )
-
-    if chain == 1:
-        return next_layers(whole, loads, coupling, schur_inv, [], False)[0]
-    finished, block = next_layers(whole, loads, coupling, schur_inv, [], True)
-    for _ in range(chain - 2):
-        block, solved, _ = later_round(exchange_all(block))
-        finished, block = next_layers(
-            exchange_row(block), loads, coupling, schur_inv, [solved], True
-        )
-    block, solved, row = later_round(exchange_all(block))
-
-    def last_round(finished, block, solved, loads, coupling, schur_inv):
-        return next_layers(exchange_row(block), loads, coupling, schur_inv, [solved], False)[0]
-
-    return lax.cond(
-        row[0] == chain - 1,
-        last_round,
-        lambda finished, *rest: finished,
-        finished, block, solved, loads, coupling, schur_inv,
-    )
+        if send:
+            block, solved, row = call(
+                functools.partial(cross_kernel, row_axis="sweep"),
+                (gathered_shape, solved_shape, row_shape),
+                (exchange_all(sent[0]), whole, received, loads, coupling, schur_inv),
+            )
+    return finished
 
 
 def solution(mesh):

time: 49.1 us -> 48.2 us (0.982)
  blocking collectives: 44.7 us -> 44 us
    all_to_all x4 -> x3, blocking collectives: 34.8 us -> 26.7 us  [exchange_row(): lax.all_to_all(blocks, 'xsec', split_axis=0, concat_axis=0, tiled=True, a...]
    all_to_all x1, blocking collectives: 9.92 us -> 17.3 us  [exchange_all(): lax.all_to_all(blocks, ('sweep', 'xsec'), split_axis=0, concat_axis=0, ti...]
    pallas_call x6 -> x5, Pallas kernels: 3.44 us -> 3.19 us  [call(): pl.pallas_call(kernel, out_shape=out_shape, in_specs=[pl.BlockSpec(memory...]
where the time goes in v8:
time: 48.2 us; the launch traced here: 47.9 us
  blocking collectives  44 us (91%)
  Pallas kernels  3.19 us (7%)
  local copies, waits for them, and re-layouts  0.63 us (1%)
    all_to_all x3, blocking collectives, exchange_row(): lax.all_to_all(blocks, 'xsec', split_axis=0, concat_axis=0, tiled=True, a...  26.7 us
    all_to_all x1, blocking collectives, exchange_all(): lax.all_to_all(blocks, ('sweep', 'xsec'), split_axis=0, concat_axis=0, ti...  17.3 us
    pallas_call x5, Pallas kernels, call(): pl.pallas_call(kernel, out_shape=out_shape, in_specs=[pl.BlockSpec(memory...  3.19 us

profile of v8, /device:TPU:4, one launch (start us, length us, event | category | flops | bytes accessed | tf_op | source)
XLA Modules:
  0.0 47.9 jit_solution(17246937645494193074)
XLA Ops:
  0.0 2.0 %shard_map.66 = (bf16[16,8,256]{2,1,0:T(8,128)(2,1)S(1)}, s32[16,192]{1,0:T(8,128)S(1)}, s32[16,192]{1,0:T(8,128)S(1)}, f32[2,2,128]{2,1,0:T(2,128)S(1)}, bf16[2,2,2048,128]{3,2,1,0:T(8,128)(2,1)S(1)}) custom-call(bf16[2,24,40,128]{3,2,1,0:T(8,128)(2,1)} %bitcast.6, bf16[2,4,40,128]{3,2,1,0:T(8,128)(2,1)} %bitcast.7, s32[16,192]{1,0:T(8,128)} %bitcast.8, ...), custom_call_target="tpu_custom_call" | custom-call | tf_op jit(solution)/shard_map/pallas_call | solution.py:249
  2.0 10.5 %all_to_all.25.received = bf16[16,8,256]{2,1,0:T(8,128)(2,1)S(1)} all-to-all(bf16[16,8,256]{2,1,0:T(8,128)(2,1)S(1)} %get-tuple-element.43), channel_id=1, replica_groups={{9,10,11,12,13,14,15,0,1,2,3,4,5,6,7,8},{25,26,27,28,29,30,31,16,17,18,..., dimensions={0} | all-to-all | bytes 131072 | tf_op jit(solution)/shard_map/all_to_all | solution.py:264
  12.5 0.4 shard_map.67
  12.9 8.1 %all_to_all.26.gathered.whole = bf16[16,8,128]{2,1,0:T(8,128)(2,1)S(1)} all-to-all(bf16[16,8,128]{2,1,0:T(8,128)(2,1)S(1)} %get-tuple-element.47), channel_id=1, replica_groups={{9,10,11,12,13,14,15,0,1,2,3,4,5,6,7,8},{25,26,27,28,29,30,31,16,17,18,..., dimensions={0} | all-to-all | bytes 65536 | tf_op jit(solution)/shard_map/all_to_all | solution.py:264
  21.0 0.3 shard_map.68
  21.3 17.3 %all_to_all.27.everyone = bf16[32,8,128]{2,1,0:T(8,128)(2,1)S(1)} all-to-all(bf16[32,8,128]{2,1,0:T(8,128)(2,1)S(1)} %get-tuple-element.53), channel_id=1, replica_groups=mesh['sweep'=2,'xsec'=16] {'sweep','xsec'}, dimensions={0} | all-to-all | bytes 131072 | tf_op jit(solution)/shard_map/all_to_all | solution.py:270
  38.6 0.3 shard_map.69
  38.9 8.3 %conditional.3 = (f32[2,8,128]{2,1,0:T(8,128)S(1)}) conditional(s32[]{:T(128)} %bitcast.5, f32[2,8,128]{2,1,0:T(8,128)S(1)} %get-tuple-element.55, (bf16[16,8,128]{2,1,0:T(8,128)(2,1)S(1)}, f32[8,128]{1,0:T(8,128)S(1)}, bf16[2,2,2048,128]{3,2,1,0:T(8,128)(2,1)S(1)}) %tuple.19), branch_computations={%region_2.0_spmd, %region_3.0_spmd} | conditional | bytes 65544 | solution.py:342
  39.0 8.1 %all_to_all.24.refs_0_ = bf16[16,8,128]{2,1,0:T(8,128)(2,1)S(1)} all-to-all(bf16[16,8,128]{2,1,0:T(8,128)(2,1)S(1)} %get-tuple-element.25), channel_id=1, replica_groups={{9,10,11,12,13,14,15,0,1,2,3,4,5,6,7,8},{25,26,27,28,29,30,31,16,17,18,..., dimensions={0} | all-to-all | bytes 65536 | tf_op jit(solution)/shard_map/cond/branch_1_fun/all_to_all | solution.py:264
  47.1 0.2 branch_1_fun.3
  47.3 0.6 %copy.15 = f32[2,8,128]{2,1,0:T(8,128)} copy(f32[2,8,128]{2,1,0:T(8,128)S(1)} %get-tuple-element.58) | data formatting | bytes 16384
  (3 shorter events, 0.1 us)

commit v9 on v8

--- a/solution.py
+++ b/solution.py
@@ -2,6 +2,7 @@
 
 import jax
 import jax.numpy as jnp
+import numpy as np
 from jax import lax
 from jax.experimental import pallas as pl
 from jax.experimental.pallas import tpu as pltpu
@@ -14,12 +15,12 @@
 BF16 = jnp.bfloat16
 
 
-def first_of(count):
-    return (count // 2 + 1) % count
+def row_order(count):
+    return [int(device) for device in np.random.RandomState(161).permutation(count)]
 
 
 def place_of(device, count):
-    return (device - first_of(count)) % count
+    return row_order(count).index(device)
 
 
 def iota(shape, axis):
@@ -259,10 +260,9 @@
 
 
 def exchange_row(blocks):
-    count = blocks.shape[0]
-    order = [(first_of(count) + place) % count for place in range(count)]
     return lax.all_to_all(
-        blocks, "xsec", split_axis=0, concat_axis=0, tiled=True, axis_index_groups=[order]
+        blocks, "xsec", split_axis=0, concat_axis=0, tiled=True,
+        axis_index_groups=[row_order(blocks.shape[0])],
     )
 
 

time: 48.2 us -> 47.8 us (level)
  blocking collectives: 44 us -> 43.4 us
    all_to_all x1, blocking collectives: 17.3 us -> 16.4 us  [exchange_all(): lax.all_to_all(blocks, ('sweep', 'xsec'), split_axis=0, concat_axis=0, ti...]
where the time goes in v9:
time: 47.8 us; the launch traced here: 47.3 us
  blocking collectives  43.4 us (91%)
  Pallas kernels  3.19 us (7%)
  local copies, waits for them, and re-layouts  0.63 us (1%)
    all_to_all x3, blocking collectives, exchange_row(): lax.all_to_all(blocks, 'xsec', split_axis=0, concat_axis=0, tiled=True, a...  26.9 us
    all_to_all x1, blocking collectives, exchange_all(): lax.all_to_all(blocks, ('sweep', 'xsec'), split_axis=0, concat_axis=0, ti...  16.4 us
    pallas_call x5, Pallas kernels, call(): pl.pallas_call(kernel, out_shape=out_shape, in_specs=[pl.BlockSpec(memory...  3.19 us

profile of v9, /device:TPU:4, one launch (start us, length us, event | category | flops | bytes accessed | tf_op | source)
XLA Modules:
  0.0 47.3 jit_solution(12979363392232104058)
XLA Ops:
  0.0 2.0 %shard_map.66 = (bf16[16,8,256]{2,1,0:T(8,128)(2,1)S(1)}, s32[16,192]{1,0:T(8,128)S(1)}, s32[16,192]{1,0:T(8,128)S(1)}, f32[2,2,128]{2,1,0:T(2,128)S(1)}, bf16[2,2,2048,128]{3,2,1,0:T(8,128)(2,1)S(1)}) custom-call(bf16[2,24,40,128]{3,2,1,0:T(8,128)(2,1)} %bitcast.6, bf16[2,4,40,128]{3,2,1,0:T(8,128)(2,1)} %bitcast.7, s32[16,192]{1,0:T(8,128)} %bitcast.8, ...), custom_call_target="tpu_custom_call" | custom-call | tf_op jit(solution)/shard_map/pallas_call | solution.py:250
  2.0 11.1 %all_to_all.25.received = bf16[16,8,256]{2,1,0:T(8,128)(2,1)S(1)} all-to-all(bf16[16,8,256]{2,1,0:T(8,128)(2,1)S(1)} %get-tuple-element.43), channel_id=1, replica_groups={{5,12,8,9,6,2,15,0,10,7,1,13,4,3,11,14},{21,28,24,25,22,18,31,16,26,23,..., dimensions={0} | all-to-all | bytes 131072 | tf_op jit(solution)/shard_map/all_to_all | solution.py:263
  13.1 0.4 shard_map.67
  13.4 7.9 %all_to_all.26.gathered.whole = bf16[16,8,128]{2,1,0:T(8,128)(2,1)S(1)} all-to-all(bf16[16,8,128]{2,1,0:T(8,128)(2,1)S(1)} %get-tuple-element.47), channel_id=1, replica_groups={{5,12,8,9,6,2,15,0,10,7,1,13,4,3,11,14},{21,28,24,25,22,18,31,16,26,23,..., dimensions={0} | all-to-all | bytes 65536 | tf_op jit(solution)/shard_map/all_to_all | solution.py:263
  21.4 0.3 shard_map.68
  21.7 16.4 %all_to_all.27.everyone = bf16[32,8,128]{2,1,0:T(8,128)(2,1)S(1)} all-to-all(bf16[32,8,128]{2,1,0:T(8,128)(2,1)S(1)} %get-tuple-element.53), channel_id=1, replica_groups=mesh['sweep'=2,'xsec'=16] {'sweep','xsec'}, dimensions={0} | all-to-all | bytes 131072 | tf_op jit(solution)/shard_map/all_to_all | solution.py:270
  38.1 0.3 shard_map.69
  38.5 8.2 %conditional.3 = (f32[2,8,128]{2,1,0:T(8,128)S(1)}) conditional(s32[]{:T(128)} %bitcast.5, f32[2,8,128]{2,1,0:T(8,128)S(1)} %get-tuple-element.55, (bf16[16,8,128]{2,1,0:T(8,128)(2,1)S(1)}, f32[8,128]{1,0:T(8,128)S(1)}, bf16[2,2,2048,128]{3,2,1,0:T(8,128)(2,1)S(1)}) %tuple.19), branch_computations={%region_2.0_spmd, %region_3.0_spmd} | conditional | bytes 65544 | solution.py:342
  38.5 7.9 %all_to_all.24.refs_0_ = bf16[16,8,128]{2,1,0:T(8,128)(2,1)S(1)} all-to-all(bf16[16,8,128]{2,1,0:T(8,128)(2,1)S(1)} %get-tuple-element.25), channel_id=1, replica_groups={{5,12,8,9,6,2,15,0,10,7,1,13,4,3,11,14},{21,28,24,25,22,18,31,16,26,23,..., dimensions={0} | all-to-all | bytes 65536 | tf_op jit(solution)/shard_map/cond/branch_1_fun/all_to_all | solution.py:263
  46.4 0.2 branch_1_fun.3
  46.7 0.6 %copy.15 = f32[2,8,128]{2,1,0:T(8,128)} copy(f32[2,8,128]{2,1,0:T(8,128)S(1)} %get-tuple-element.58) | data formatting | bytes 16384
  (3 shorter events, 0.1 us)

commit v10 on v9

--- a/solution.py
+++ b/solution.py
@@ -11,6 +11,7 @@
 CAP = 8
 LANES = 128
 CHUNKS = 2
+DEPTH = 256
 F32 = jnp.float32
 BF16 = jnp.bfloat16
 
@@ -158,10 +159,23 @@
     layers, _, width = loads.shape
     place = iota((width, face_rows), 0)
     total = jnp.zeros((layers * rows, width), F32)
-    for sender in range(peers):
-        onehot = jnp.where(place == place_rows[sender : sender + 1, :], 1.0, 0.0).astype(BF16)
-        values = received[place_of(sender, peers)].astype(F32)[:, :face_rows]
-        layer_row = layer_rows[sender : sender + 1, :]
+    whole_tiles = face_rows // LANES * LANES
+    pieces = [(sender, at, LANES) for sender in range(peers) for at in range(0, whole_tiles, LANES)]
+    pieces += [(sender, whole_tiles, face_rows - whole_tiles) for sender in range(peers) if face_rows > whole_tiles]
+    place = iota((width, DEPTH), 0)
+    while pieces:
+        group = []
+        while pieces and sum(piece[2] for piece in group) + pieces[0][2] <= DEPTH:
+            group.append(pieces.pop(0))
+        values, places, layer_row = [], [], []
+        for sender, at, size in group:
+            lanes = slice(at, at + size)
+            values.append(received[place_of(sender, peers)].astype(F32)[:, lanes])
+            places.append(place_rows[sender : sender + 1, :][:, lanes])
+            layer_row.append(layer_rows[sender : sender + 1, :][:, lanes])
+        values = jnp.concatenate(values, 1)
+        layer_row = jnp.concatenate(layer_row, 1)
+        onehot = jnp.where(place[:, : values.shape[1]] == jnp.concatenate(places, 1), 1.0, 0.0).astype(BF16)
         split = [jnp.where(layer_row == layer, values, 0.0) for layer in range(layers)]
         total += lax.dot_general(
             jnp.concatenate(split, 0).astype(BF16), onehot, (((1,), (1,)), ((), ())), preferred_element_type=F32

time: 47.8 us -> 47.8 us (level)
  no operation moved by 1% of the time
where the time goes in v10:
time: 47.8 us; the launch traced here: 47.2 us
  blocking collectives  43.4 us (91%)
  Pallas kernels  3.13 us (7%)
  local copies, waits for them, and re-layouts  0.63 us (1%)
    all_to_all x3, blocking collectives, exchange_row(): lax.all_to_all(blocks, 'xsec', split_axis=0, concat_axis=0, tiled=True, a...  26.9 us
    all_to_all x1, blocking collectives, exchange_all(): lax.all_to_all(blocks, ('sweep', 'xsec'), split_axis=0, concat_axis=0, ti...  16.4 us
    pallas_call x5, Pallas kernels, call(): pl.pallas_call(kernel, out_shape=out_shape, in_specs=[pl.BlockSpec(memory...  3.13 us

profile of v10, /device:TPU:4, one launch (start us, length us, event | category | flops | bytes accessed | tf_op | source)
XLA Modules:
  0.0 47.2 jit_solution(7629699156390197973)
XLA Ops:
  0.0 2.0 %shard_map.66 = (bf16[16,8,256]{2,1,0:T(8,128)(2,1)S(1)}, s32[16,192]{1,0:T(8,128)S(1)}, s32[16,192]{1,0:T(8,128)S(1)}, f32[2,2,128]{2,1,0:T(2,128)S(1)}, bf16[2,2,2048,128]{3,2,1,0:T(8,128)(2,1)S(1)}) custom-call(bf16[2,24,40,128]{3,2,1,0:T(8,128)(2,1)} %bitcast.6, bf16[2,4,40,128]{3,2,1,0:T(8,128)(2,1)} %bitcast.7, s32[16,192]{1,0:T(8,128)} %bitcast.8, ...), custom_call_target="tpu_custom_call" | custom-call | tf_op jit(solution)/shard_map/pallas_call | solution.py:264
  2.0 11.1 %all_to_all.25.received = bf16[16,8,256]{2,1,0:T(8,128)(2,1)S(1)} all-to-all(bf16[16,8,256]{2,1,0:T(8,128)(2,1)S(1)} %get-tuple-element.43), channel_id=1, replica_groups={{5,12,8,9,6,2,15,0,10,7,1,13,4,3,11,14},{21,28,24,25,22,18,31,16,26,23,..., dimensions={0} | all-to-all | bytes 131072 | tf_op jit(solution)/shard_map/all_to_all | solution.py:277
  13.1 0.3 shard_map.67
  13.4 7.9 %all_to_all.26.gathered.whole = bf16[16,8,128]{2,1,0:T(8,128)(2,1)S(1)} all-to-all(bf16[16,8,128]{2,1,0:T(8,128)(2,1)S(1)} %get-tuple-element.47), channel_id=1, replica_groups={{5,12,8,9,6,2,15,0,10,7,1,13,4,3,11,14},{21,28,24,25,22,18,31,16,26,23,..., dimensions={0} | all-to-all | bytes 65536 | tf_op jit(solution)/shard_map/all_to_all | solution.py:277
  21.3 0.3 shard_map.68
  21.6 16.4 %all_to_all.27.everyone = bf16[32,8,128]{2,1,0:T(8,128)(2,1)S(1)} all-to-all(bf16[32,8,128]{2,1,0:T(8,128)(2,1)S(1)} %get-tuple-element.53), channel_id=1, replica_groups=mesh['sweep'=2,'xsec'=16] {'sweep','xsec'}, dimensions={0} | all-to-all | bytes 131072 | tf_op jit(solution)/shard_map/all_to_all | solution.py:284
  38.1 0.3 shard_map.69
  38.4 8.2 %conditional.3 = (f32[2,8,128]{2,1,0:T(8,128)S(1)}) conditional(s32[]{:T(128)} %bitcast.5, f32[2,8,128]{2,1,0:T(8,128)S(1)} %get-tuple-element.55, (bf16[16,8,128]{2,1,0:T(8,128)(2,1)S(1)}, f32[8,128]{1,0:T(8,128)S(1)}, bf16[2,2,2048,128]{3,2,1,0:T(8,128)(2,1)S(1)}) %tuple.19), branch_computations={%region_2.0_spmd, %region_3.0_spmd} | conditional | bytes 65544 | solution.py:356
  38.4 7.9 %all_to_all.24.refs_0_ = bf16[16,8,128]{2,1,0:T(8,128)(2,1)S(1)} all-to-all(bf16[16,8,128]{2,1,0:T(8,128)(2,1)S(1)} %get-tuple-element.25), channel_id=1, replica_groups={{5,12,8,9,6,2,15,0,10,7,1,13,4,3,11,14},{21,28,24,25,22,18,31,16,26,23,..., dimensions={0} | all-to-all | bytes 65536 | tf_op jit(solution)/shard_map/cond/branch_1_fun/all_to_all | solution.py:277
  46.3 0.2 branch_1_fun.3
  46.6 0.6 %copy.15 = f32[2,8,128]{2,1,0:T(8,128)} copy(f32[2,8,128]{2,1,0:T(8,128)S(1)} %get-tuple-element.58) | data formatting | bytes 16384
  (3 shorter events, 0.1 us)

commit v11 on v10

--- a/solution.py
+++ b/solution.py
@@ -207,10 +207,9 @@
     return jnp.concatenate([first[:half] - second[half:], second[:half] + first[half:]], 0)
 
 
-def cross_kernel(everyone, whole, received, loads, coupling, schur, out, solved_out, row_out, *, row_axis):
+def cross_kernel(everyone, whole, pairs, loads, coupling, schur, out, solved_out, row_out, *, row_axis):
     peers = whole.shape[0]
     _, count, width = loads.shape
-    spare = received.shape[2] - 4 * width // count
     row = lax.axis_index(row_axis)
     row_out[0] = row
     start = jnp.maximum(row - 1, 0) * peers
@@ -218,9 +217,8 @@
     blocks = []
     for peer in range(peers):
         place = place_of(peer, peers)
-        pair = unpack_coupling(received[place].astype(F32)[:, spare:])
         before = everyone[start + peer].astype(F32) * keep
-        blocks.append(couple(whole[place].astype(F32), pair, before).astype(BF16))
+        blocks.append(couple(whole[place].astype(F32), pairs[peer], before).astype(BF16))
     solved = apply_schur(jnp.concatenate(blocks, 1), schur, 0)
     solved_out[...] = solved
     block = couple(loads[1], coupling[1], solved).astype(BF16)
@@ -233,9 +231,24 @@
     return jnp.concatenate([gathered[place_of(peer, count)] for peer in range(count)], 1)
 
 
-def layer_kernel(gathered, loads, coupling, schur, out, solved_out, *row_out, layer):
-    if row_out:
-        row_out[0][0] = lax.axis_index("sweep")
+def start_kernel(gathered, received, loads, coupling, schur, out, solved_out, row_out, pairs):
+    row = lax.axis_index("sweep")
+    row_out[0] = row
+    layer_kernel(gathered, loads, coupling, schur, out, solved_out, layer=0)
+
+    @pl.when(row == 0)
+    def _():
+        pairs[...] = jnp.zeros(pairs.shape, F32)
+
+    @pl.when(row > 0)
+    def _():
+        peers, count, lanes = received.shape
+        spare = lanes - 4 * pairs.shape[2] // count
+        for peer in range(peers):
+            pairs[peer] = unpack_coupling(received[place_of(peer, peers)].astype(F32)[:, spare:])
+
+
+def layer_kernel(gathered, loads, coupling, schur, out, solved_out, *, layer):
     rhs = side_by_side(gathered)
     solved = apply_schur(rhs, schur, layer)
     solved_out[...] = solved
@@ -344,10 +357,10 @@
             (exchange_row(block), *done, schur_inv),
         )
 
-    block, solved, row = call(
-        functools.partial(layer_kernel, layer=0),
-        (gathered_shape, solved_shape, row_shape),
-        (whole, loads, coupling, schur_inv),
+    block, solved, row, pairs = call(
+        start_kernel,
+        (gathered_shape, solved_shape, row_shape, struct((peers, 2, width), F32)),
+        (whole, received, loads, coupling, schur_inv),
     )
     finished = loads
     for round_at in range(chain):
@@ -363,7 +376,7 @@
             block, solved, row = call(
                 functools.partial(cross_kernel, row_axis="sweep"),
                 (gathered_shape, solved_shape, row_shape),
-                (exchange_all(sent[0]), whole, received, loads, coupling, schur_inv),
+                (exchange_all(sent[0]), whole, pairs, loads, coupling, schur_inv),
             )
     return finished
 

time: 47.8 us -> 47.7 us (level)
  no operation moved by 1% of the time
where the time goes in v11:
time: 47.7 us; the launch traced here: 47.1 us
  blocking collectives  43.3 us (91%)
  Pallas kernels  3.15 us (7%)
  local copies, waits for them, and re-layouts  0.63 us (1%)
    all_to_all x3, blocking collectives, exchange_row(): lax.all_to_all(blocks, 'xsec', split_axis=0, concat_axis=0, tiled=True, a...  26.9 us
    all_to_all x1, blocking collectives, exchange_all(): lax.all_to_all(blocks, ('sweep', 'xsec'), split_axis=0, concat_axis=0, ti...  16.3 us
    pallas_call x5, Pallas kernels, call(): pl.pallas_call(kernel, out_shape=out_shape, in_specs=[pl.BlockSpec(memory...  3.15 us

profile of v11, /device:TPU:4, one launch (start us, length us, event | category | flops | bytes accessed | tf_op | source)
XLA Modules:
  0.0 47.1 jit_solution(2294205320561923512)
XLA Ops:
  0.0 2.0 %shard_map.66 = (bf16[16,8,256]{2,1,0:T(8,128)(2,1)S(1)}, s32[16,192]{1,0:T(8,128)S(1)}, s32[16,192]{1,0:T(8,128)S(1)}, f32[2,2,128]{2,1,0:T(2,128)S(1)}, bf16[2,2,2048,128]{3,2,1,0:T(8,128)(2,1)S(1)}) custom-call(bf16[2,24,40,128]{3,2,1,0:T(8,128)(2,1)} %bitcast.6, bf16[2,4,40,128]{3,2,1,0:T(8,128)(2,1)} %bitcast.7, s32[16,192]{1,0:T(8,128)} %bitcast.8, ...), custom_call_target="tpu_custom_call" | custom-call | tf_op jit(solution)/shard_map/pallas_call | solution.py:277
  2.0 11.1 %all_to_all.25.received = bf16[16,8,256]{2,1,0:T(8,128)(2,1)S(1)} all-to-all(bf16[16,8,256]{2,1,0:T(8,128)(2,1)S(1)} %get-tuple-element.44), channel_id=1, replica_groups={{5,12,8,9,6,2,15,0,10,7,1,13,4,3,11,14},{21,28,24,25,22,18,31,16,26,23,..., dimensions={0} | all-to-all | bytes 131072 | tf_op jit(solution)/shard_map/all_to_all | solution.py:290
  13.1 0.3 shard_map.67
  13.4 7.9 %all_to_all.26.gathered.whole = bf16[16,8,128]{2,1,0:T(8,128)(2,1)S(1)} all-to-all(bf16[16,8,128]{2,1,0:T(8,128)(2,1)S(1)} %get-tuple-element.48), channel_id=1, replica_groups={{5,12,8,9,6,2,15,0,10,7,1,13,4,3,11,14},{21,28,24,25,22,18,31,16,26,23,..., dimensions={0} | all-to-all | bytes 65536 | tf_op jit(solution)/shard_map/all_to_all | solution.py:290
  21.3 0.3 shard_map.68
  21.7 16.3 %all_to_all.27.everyone = bf16[32,8,128]{2,1,0:T(8,128)(2,1)S(1)} all-to-all(bf16[32,8,128]{2,1,0:T(8,128)(2,1)S(1)} %get-tuple-element.54), channel_id=1, replica_groups=mesh['sweep'=2,'xsec'=16] {'sweep','xsec'}, dimensions={0} | all-to-all | bytes 131072 | tf_op jit(solution)/shard_map/all_to_all | solution.py:297
  38.1 0.3 shard_map.69
  38.3 8.2 %conditional.3 = (f32[2,8,128]{2,1,0:T(8,128)S(1)}) conditional(s32[]{:T(128)} %bitcast.5, f32[2,8,128]{2,1,0:T(8,128)S(1)} %get-tuple-element.57, (bf16[16,8,128]{2,1,0:T(8,128)(2,1)S(1)}, f32[8,128]{1,0:T(8,128)S(1)}, bf16[2,2,2048,128]{3,2,1,0:T(8,128)(2,1)S(1)}) %tuple.19), branch_computations={%region_2.0_spmd, %region_3.0_spmd} | conditional | bytes 65544 | solution.py:369
  38.3 7.9 %all_to_all.24.refs_0_ = bf16[16,8,128]{2,1,0:T(8,128)(2,1)S(1)} all-to-all(bf16[16,8,128]{2,1,0:T(8,128)(2,1)S(1)} %get-tuple-element.25), channel_id=1, replica_groups={{5,12,8,9,6,2,15,0,10,7,1,13,4,3,11,14},{21,28,24,25,22,18,31,16,26,23,..., dimensions={0} | all-to-all | bytes 65536 | tf_op jit(solution)/shard_map/cond/branch_1_fun/all_to_all | solution.py:290
  46.3 0.2 branch_1_fun.3
  46.5 0.6 %copy.15 = f32[2,8,128]{2,1,0:T(8,128)} copy(f32[2,8,128]{2,1,0:T(8,128)S(1)} %get-tuple-element.60) | data formatting | bytes 16384
  (3 shorter events, 0.1 us)

commit v12 on v11

--- a/solution.py
+++ b/solution.py
@@ -10,7 +10,7 @@
 
 CAP = 8
 LANES = 128
-CHUNKS = 2
+CHUNKS = 1
 DEPTH = 256
 F32 = jnp.float32
 BF16 = jnp.bfloat16

time: 47.7 us -> 47.6 us (level)
  no operation moved by 1% of the time
where the time goes in v12:
time: 47.6 us; the launch traced here: 47.1 us
  blocking collectives  43.3 us (91%)
  Pallas kernels  3.12 us (7%)
  local copies, waits for them, and re-layouts  0.63 us (1%)
    all_to_all x3, blocking collectives, exchange_row(): lax.all_to_all(blocks, 'xsec', split_axis=0, concat_axis=0, tiled=True, a...  26.9 us
    all_to_all x1, blocking collectives, exchange_all(): lax.all_to_all(blocks, ('sweep', 'xsec'), split_axis=0, concat_axis=0, ti...  16.3 us
    pallas_call x5, Pallas kernels, call(): pl.pallas_call(kernel, out_shape=out_shape, in_specs=[pl.BlockSpec(memory...  3.12 us

profile of v12, /device:TPU:4, one launch (start us, length us, event | category | flops | bytes accessed | tf_op | source)
XLA Modules:
  0.0 47.1 jit_solution(7521062482822874858)
XLA Ops:
  0.0 2.0 %shard_map.66 = (bf16[16,8,256]{2,1,0:T(8,128)(2,1)S(1)}, s32[16,192]{1,0:T(8,128)S(1)}, s32[16,192]{1,0:T(8,128)S(1)}, f32[2,2,128]{2,1,0:T(2,128)S(1)}, bf16[2,2,2048,128]{3,2,1,0:T(8,128)(2,1)S(1)}) custom-call(bf16[2,24,40,128]{3,2,1,0:T(8,128)(2,1)} %bitcast.6, bf16[2,4,40,128]{3,2,1,0:T(8,128)(2,1)} %bitcast.7, s32[16,192]{1,0:T(8,128)} %bitcast.8, ...), custom_call_target="tpu_custom_call" | custom-call | tf_op jit(solution)/shard_map/pallas_call | solution.py:277
  2.0 11.1 %all_to_all.25.received = bf16[16,8,256]{2,1,0:T(8,128)(2,1)S(1)} all-to-all(bf16[16,8,256]{2,1,0:T(8,128)(2,1)S(1)} %get-tuple-element.44), channel_id=1, replica_groups={{5,12,8,9,6,2,15,0,10,7,1,13,4,3,11,14},{21,28,24,25,22,18,31,16,26,23,..., dimensions={0} | all-to-all | bytes 131072 | tf_op jit(solution)/shard_map/all_to_all | solution.py:290
  13.0 0.3 shard_map.67
  13.3 7.9 %all_to_all.26.gathered.whole = bf16[16,8,128]{2,1,0:T(8,128)(2,1)S(1)} all-to-all(bf16[16,8,128]{2,1,0:T(8,128)(2,1)S(1)} %get-tuple-element.48), channel_id=1, replica_groups={{5,12,8,9,6,2,15,0,10,7,1,13,4,3,11,14},{21,28,24,25,22,18,31,16,26,23,..., dimensions={0} | all-to-all | bytes 65536 | tf_op jit(solution)/shard_map/all_to_all | solution.py:290
  21.3 0.3 shard_map.68
  21.7 16.3 %all_to_all.27.everyone = bf16[32,8,128]{2,1,0:T(8,128)(2,1)S(1)} all-to-all(bf16[32,8,128]{2,1,0:T(8,128)(2,1)S(1)} %get-tuple-element.54), channel_id=1, replica_groups=mesh['sweep'=2,'xsec'=16] {'sweep','xsec'}, dimensions={0} | all-to-all | bytes 131072 | tf_op jit(solution)/shard_map/all_to_all | solution.py:297
  38.0 0.3 shard_map.69
  38.3 8.2 %conditional.3 = (f32[2,8,128]{2,1,0:T(8,128)S(1)}) conditional(s32[]{:T(128)} %bitcast.5, f32[2,8,128]{2,1,0:T(8,128)S(1)} %get-tuple-element.57, (bf16[16,8,128]{2,1,0:T(8,128)(2,1)S(1)}, f32[8,128]{1,0:T(8,128)S(1)}, bf16[2,2,2048,128]{3,2,1,0:T(8,128)(2,1)S(1)}) %tuple.19), branch_computations={%region_2.0_spmd, %region_3.0_spmd} | conditional | bytes 65544 | solution.py:369
  38.3 7.9 %all_to_all.24.refs_0_ = bf16[16,8,128]{2,1,0:T(8,128)(2,1)S(1)} all-to-all(bf16[16,8,128]{2,1,0:T(8,128)(2,1)S(1)} %get-tuple-element.25), channel_id=1, replica_groups={{5,12,8,9,6,2,15,0,10,7,1,13,4,3,11,14},{21,28,24,25,22,18,31,16,26,23,..., dimensions={0} | all-to-all | bytes 65536 | tf_op jit(solution)/shard_map/cond/branch_1_fun/all_to_all | solution.py:290
  46.2 0.2 branch_1_fun.3
  46.5 0.6 %copy.15 = f32[2,8,128]{2,1,0:T(8,128)} copy(f32[2,8,128]{2,1,0:T(8,128)S(1)} %get-tuple-element.60) | data formatting | bytes 16384
  (3 shorter events, 0.1 us)

commit v13 on v12

--- a/solution.py
+++ b/solution.py
@@ -17,7 +17,7 @@
 
 
 def row_order(count):
-    return [int(device) for device in np.random.RandomState(161).permutation(count)]
+    return [int(device) for device in np.random.RandomState(2312).permutation(count)]
 
 
 def place_of(device, count):

time: 47.6 us -> 47.5 us (level)
  no operation moved by 1% of the time
where the time goes in v13:
time: 47.5 us; the launch traced here: 47 us
  blocking collectives  43.2 us (91%)
  Pallas kernels  3.12 us (7%)
  local copies, waits for them, and re-layouts  0.63 us (1%)
    all_to_all x3, blocking collectives, exchange_row(): lax.all_to_all(blocks, 'xsec', split_axis=0, concat_axis=0, tiled=True, a...  26.8 us
    all_to_all x1, blocking collectives, exchange_all(): lax.all_to_all(blocks, ('sweep', 'xsec'), split_axis=0, concat_axis=0, ti...  16.3 us
    pallas_call x5, Pallas kernels, call(): pl.pallas_call(kernel, out_shape=out_shape, in_specs=[pl.BlockSpec(memory...  3.12 us

profile of v13, /device:TPU:4, one launch (start us, length us, event | category | flops | bytes accessed | tf_op | source)
XLA Modules:
  0.0 47.0 jit_solution(10495311552619559184)
XLA Ops:
  0.0 2.0 %shard_map.66 = (bf16[16,8,256]{2,1,0:T(8,128)(2,1)S(1)}, s32[16,192]{1,0:T(8,128)S(1)}, s32[16,192]{1,0:T(8,128)S(1)}, f32[2,2,128]{2,1,0:T(2,128)S(1)}, bf16[2,2,2048,128]{3,2,1,0:T(8,128)(2,1)S(1)}) custom-call(bf16[2,24,40,128]{3,2,1,0:T(8,128)(2,1)} %bitcast.6, bf16[2,4,40,128]{3,2,1,0:T(8,128)(2,1)} %bitcast.7, s32[16,192]{1,0:T(8,128)} %bitcast.8, ...), custom_call_target="tpu_custom_call" | custom-call | tf_op jit(solution)/shard_map/pallas_call | solution.py:277
  2.0 11.0 %all_to_all.25.received = bf16[16,8,256]{2,1,0:T(8,128)(2,1)S(1)} all-to-all(bf16[16,8,256]{2,1,0:T(8,128)(2,1)S(1)} %get-tuple-element.44), channel_id=1, replica_groups={{5,14,8,1,6,3,9,12,13,0,11,2,15,10,7,4},{21,30,24,17,22,19,25,28,29,16,..., dimensions={0} | all-to-all | bytes 131072 | tf_op jit(solution)/shard_map/all_to_all | solution.py:290
  12.9 0.3 shard_map.67
  13.3 8.0 %all_to_all.26.gathered.whole = bf16[16,8,128]{2,1,0:T(8,128)(2,1)S(1)} all-to-all(bf16[16,8,128]{2,1,0:T(8,128)(2,1)S(1)} %get-tuple-element.48), channel_id=1, replica_groups={{5,14,8,1,6,3,9,12,13,0,11,2,15,10,7,4},{21,30,24,17,22,19,25,28,29,16,..., dimensions={0} | all-to-all | bytes 65536 | tf_op jit(solution)/shard_map/all_to_all | solution.py:290
  21.2 0.3 shard_map.68
  21.6 16.3 %all_to_all.27.everyone = bf16[32,8,128]{2,1,0:T(8,128)(2,1)S(1)} all-to-all(bf16[32,8,128]{2,1,0:T(8,128)(2,1)S(1)} %get-tuple-element.54), channel_id=1, replica_groups=mesh['sweep'=2,'xsec'=16] {'sweep','xsec'}, dimensions={0} | all-to-all | bytes 131072 | tf_op jit(solution)/shard_map/all_to_all | solution.py:297
  38.0 0.3 shard_map.69
  38.2 8.1 %conditional.3 = (f32[2,8,128]{2,1,0:T(8,128)S(1)}) conditional(s32[]{:T(128)} %bitcast.5, f32[2,8,128]{2,1,0:T(8,128)S(1)} %get-tuple-element.57, (bf16[16,8,128]{2,1,0:T(8,128)(2,1)S(1)}, f32[8,128]{1,0:T(8,128)S(1)}, bf16[2,2,2048,128]{3,2,1,0:T(8,128)(2,1)S(1)}) %tuple.19), branch_computations={%region_2.0_spmd, %region_3.0_spmd} | conditional | bytes 65544 | solution.py:369
  38.3 7.9 %all_to_all.24.refs_0_ = bf16[16,8,128]{2,1,0:T(8,128)(2,1)S(1)} all-to-all(bf16[16,8,128]{2,1,0:T(8,128)(2,1)S(1)} %get-tuple-element.25), channel_id=1, replica_groups={{5,14,8,1,6,3,9,12,13,0,11,2,15,10,7,4},{21,30,24,17,22,19,25,28,29,16,..., dimensions={0} | all-to-all | bytes 65536 | tf_op jit(solution)/shard_map/cond/branch_1_fun/all_to_all | solution.py:290
  46.1 0.2 branch_1_fun.3
  46.4 0.6 %copy.15 = f32[2,8,128]{2,1,0:T(8,128)} copy(f32[2,8,128]{2,1,0:T(8,128)S(1)} %get-tuple-element.60) | data formatting | bytes 16384
  (3 shorter events, 0.1 us)
